TPU v7x, 128 devices: a whole 4x4x4 slice. The times are simulated.
128 devices in a mesh: batch: 64 (over x, y_hi, z, core), seq: 2 (over y_lo).
Axes of the slice: x: 4, y: 4 (y_hi: 2, y_lo: 2; y = y_hi * 2 + y_lo), z: 4, core: 2. Of those that a mesh axis runs over, the one named last changes fastest.
Arguments:
- tokens: bfloat16 [64, 4, 64, 768], P('batch', None, 'seq'), may hold values from -6 to 6
- segment_counts: int32 [64], P('batch'), may hold values from 1 to 4, as said below
- ln1_gain: bfloat16 [768], P(('batch', 'seq')), may hold values from 0.5 to 1.5
- ln1_bias: bfloat16 [768], P(('batch', 'seq')), may hold values from -1.75 to 1.75
- w_qkv: bfloat16 [768, 2304], P(('batch', 'seq')), may hold values from -0.21875 to 0.21875
- q_bias: bfloat16 [768], P(('batch', 'seq')), may hold values from -3 to 3
- v_bias: bfloat16 [768], P(('batch', 'seq')), may hold values from -3 to 3
- w_out: bfloat16 [768, 768], P(('batch', 'seq')), may hold values from -1.25 to 1.25
- out_bias: bfloat16 [768], P(('batch', 'seq')), may hold values from -1.75 to 1.75
- ln2_gain: bfloat16 [768], P(('batch', 'seq')), may hold values from 0.5 to 1.5
- ln2_bias: bfloat16 [768], P(('batch', 'seq')), may hold values from -1.75 to 1.75
- w_up: bfloat16 [768, 3072], P(('batch', 'seq')), may hold values from -0.21875 to 0.21875
- up_bias: bfloat16 [3072], P(('batch', 'seq')), may hold values from -3 to 3
- w_down: bfloat16 [3072, 768], P(('batch', 'seq')), may hold values from -0.109375 to 0.109375
- down_bias: bfloat16 [768], P(('batch', 'seq')), may hold values from -1.75 to 1.75
- cotangent: bfloat16 [64, 4, 64, 768], P('batch', None, 'seq'), may hold values from -6 to 6
Outputs:
- block_out: bfloat16 [64, 4, 64, 768], P('batch', None, 'seq')
- grad_tokens: bfloat16 [64, 4, 64, 768], P('batch', None, 'seq')
- grad_ln1_gain: float32 [768], P(('batch', 'seq'))
- grad_ln1_bias: float32 [768], P(('batch', 'seq'))
- grad_w_qkv: float32 [768, 2304], P(('batch', 'seq'))
- grad_q_bias: float32 [768], P(('batch', 'seq'))
- grad_v_bias: float32 [768], P(('batch', 'seq'))
- grad_w_out: float32 [768, 768], P(('batch', 'seq'))
- grad_out_bias: float32 [768], P(('batch', 'seq'))
- grad_ln2_gain: float32 [768], P(('batch', 'seq'))
- grad_ln2_bias: float32 [768], P(('batch', 'seq'))
- grad_w_up: float32 [768, 3072], P(('batch', 'seq'))
- grad_up_bias: float32 [3072], P(('batch', 'seq'))
- grad_w_down: float32 [3072, 768], P(('batch', 'seq'))
- grad_down_bias: float32 [768], P(('batch', 'seq'))
Inputs may be any that keep to these rules, and one draw needn't show every extreme that they name: `segment_counts`: slots at or beyond an item's count are absent. Some item holds 4 segments and some item holds one.
All inputs are finite; a program needn't handle non-finite values.
Results may differ from a plain program's by a relative error of at most 0.015.
Values may be sent and summed in bfloat16 or wider, within the bound.
No kernel may reach another device: no remote copies, remote signals or barrier semaphores. Data moves between devices by JAX's collectives and lax.ppermute only.
A program may use at most 128 MiB of HBM per device.

v0:
```python
import jax
import jax.numpy as jnp
from jax import lax
from jax.sharding import PartitionSpec as P

HEAD = 64
NSUM = 16


EPSILON = 1e-05
MASKED = -1e30


def passed_along(array, axis, by):
    size = lax.axis_size(axis)
    pairs = [(i, i + by) for i in range(size) if 0 <= i + by < size]
    return lax.ppermute(array, axis, pairs)


def from_root(value, axis, source):
    kept = jnp.where(lax.axis_index(axis) == source, value, 0).astype(value.dtype)
    return lax.psum(kept, axis)


def norm_rows(values, gain, shift):
    center = values - jnp.mean(values, axis=-1, keepdims=True)
    spread = jnp.mean(center * center, axis=-1, keepdims=True)
    return center * lax.rsqrt(spread + EPSILON) * gain + shift


def mat_dot(left, right):
    return jnp.dot(left, right, preferred_element_type=jnp.float32)


def left_dot(left, right):
    return lax.dot_general(
        left, right, (((0,), (0,)), ((), ())), preferred_element_type=jnp.float32
    )


def right_dot(left, right):
    return lax.dot_general(
        left, right, (((1,), (1,)), ((), ())), preferred_element_type=jnp.float32
    )


def gelu_exact(values):
    return jax.nn.gelu(values, approximate=False)


def column_total(values):
    return jnp.sum(values.astype(jnp.float32), axis=0)


def shards(
    tokens,
    segment_counts,
    ln1_gain,
    ln1_bias,
    w_qkv,
    q_bias,
    v_bias,
    w_out,
    out_bias,
    ln2_gain,
    ln2_bias,
    w_up,
    up_bias,
    w_down,
    down_bias,
    cotangent,
):
    items, slots, half, width = tokens.shape
    heads = width // HEAD
    count_rows = items * slots * half
    own_len = slots * half
    summ_len = slots * NSUM
    summary_start = half - NSUM
    scale = HEAD ** (-0.5)
    seq_index = lax.axis_index("seq")
    token_rows = tokens.reshape(count_rows, width).astype(jnp.float32)
    gain_one, bias_one, qkv_weight, query_bias, value_bias, out_weight, out_shift = (
        lax.all_gather(ln1_gain, ("batch", "seq"), axis=0, tiled=True),
        lax.all_gather(ln1_bias, ("batch", "seq"), axis=0, tiled=True),
        lax.all_gather(w_qkv, ("batch", "seq"), axis=0, tiled=True),
        lax.all_gather(q_bias, ("batch", "seq"), axis=0, tiled=True),
        lax.all_gather(v_bias, ("batch", "seq"), axis=0, tiled=True),
        lax.all_gather(w_out, ("batch", "seq"), axis=0, tiled=True),
        lax.all_gather(out_bias, ("batch", "seq"), axis=0, tiled=True),
    )
    gain_one_f = gain_one.astype(jnp.float32)
    bias_one_f = bias_one.astype(jnp.float32)
    normed_low = norm_rows(token_rows, gain_one_f, bias_one_f).astype(jnp.bfloat16)
    qkv_shift = jnp.concatenate([query_bias, jnp.zeros_like(query_bias), value_bias]).astype(
        jnp.float32
    )
    merged = (mat_dot(normed_low, qkv_weight) + qkv_shift).astype(jnp.bfloat16)
    key_own = merged[:, width : 2 * width]
    value_own = merged[:, 2 * width :]

    def summary_part(values):
        return values.reshape(items, slots, half, width)[:, :, summary_start:].reshape(
            items * summ_len, width
        )

    key_early, value_early = passed_along((key_own, value_own), "seq", 1)
    key_summ, value_summ = (
        from_root(summary_part(key_own), "seq", lax.axis_size("seq") - 1),
        from_root(summary_part(value_own), "seq", lax.axis_size("seq") - 1),
    )

    def per_item(values, length):
        return values.reshape(items, length, heads, HEAD)

    query_items = per_item(merged[:, :width], own_len)
    keys_all = jnp.concatenate(
        [per_item(key_own, own_len), per_item(key_early, own_len), per_item(key_summ, summ_len)],
        axis=1,
    )
    values_all = jnp.concatenate(
        [
            per_item(value_own, own_len),
            per_item(value_early, own_len),
            per_item(value_summ, summ_len),
        ],
        axis=1,
    )
    query_slot = jnp.arange(own_len) // half
    query_pos = jnp.arange(own_len) % half
    summ_slot = jnp.arange(summ_len) // NSUM
    slot_match = query_slot[:, None] == query_slot[None, :]
    own_allowed = slot_match & (query_pos[None, :] <= query_pos[:, None])
    early_allowed = slot_match & (seq_index >= 1)
    summ_allowed = summ_slot[None, :] < query_slot[:, None]
    allowed = jnp.concatenate([own_allowed, early_allowed, summ_allowed], axis=1)
    summ_live = summ_slot[None, :] >= query_slot[:, None] - 2
    live_pairs = jnp.concatenate([jnp.ones((own_len, 2 * own_len), bool), summ_live], axis=1)

    def score_of():
        raw = (
            jnp.einsum("nqhe,nkhe->nhqk", query_items, keys_all, preferred_element_type=jnp.float32)
            * scale
        )
        return jnp.where(allowed[None, None], raw, MASKED)

    scores = score_of()
    row_top = jnp.max(scores, axis=-1, keepdims=True)
    log_total = row_top + jnp.log(jnp.sum(jnp.exp(scores - row_top), axis=-1, keepdims=True))
    probs_low = jnp.exp(scores - log_total).astype(jnp.bfloat16)
    mixed = jnp.einsum("nhqk,nkhe->nqhe", probs_low, values_all, preferred_element_type=jnp.float32)
    mixed_low = mixed.reshape(count_rows, width).astype(jnp.bfloat16)
    hidden = token_rows + mat_dot(mixed_low, out_weight) + out_shift.astype(jnp.float32)
    gain_two, bias_two, up_weight, up_shift, down_weight, down_shift = (
        lax.all_gather(ln2_gain, ("batch", "seq"), axis=0, tiled=True),
        lax.all_gather(ln2_bias, ("batch", "seq"), axis=0, tiled=True),
        lax.all_gather(w_up, ("batch", "seq"), axis=0, tiled=True),
        lax.all_gather(up_bias, ("batch", "seq"), axis=0, tiled=True),
        lax.all_gather(w_down, ("batch", "seq"), axis=0, tiled=True),
        lax.all_gather(down_bias, ("batch", "seq"), axis=0, tiled=True),
    )
    normed_two_low = norm_rows(
        hidden, gain_two.astype(jnp.float32), bias_two.astype(jnp.float32)
    ).astype(jnp.bfloat16)
    upward = mat_dot(normed_two_low, up_weight) + up_shift.astype(jnp.float32)
    active_low = gelu_exact(upward).astype(jnp.bfloat16)
    branch = mat_dot(active_low, down_weight) + down_shift.astype(jnp.float32)
    present = (jnp.arange(slots)[None, :] < segment_counts[:, None]).astype(jnp.float32)
    present_rows = jnp.broadcast_to(present[:, :, None], (items, slots, half)).reshape(
        count_rows, 1
    )
    block_out = ((hidden + branch) * present_rows).astype(jnp.bfloat16).reshape(tokens.shape)
    grad_out = cotangent.reshape(count_rows, width).astype(jnp.float32) * present_rows
    grad_branch = grad_out.astype(jnp.bfloat16)
    gain_two, bias_two, up_weight, up_shift, down_weight, down_shift = (
        lax.all_gather(ln2_gain, ("batch", "seq"), axis=0, tiled=True),
        lax.all_gather(ln2_bias, ("batch", "seq"), axis=0, tiled=True),
        lax.all_gather(w_up, ("batch", "seq"), axis=0, tiled=True),
        lax.all_gather(up_bias, ("batch", "seq"), axis=0, tiled=True),
        lax.all_gather(w_down, ("batch", "seq"), axis=0, tiled=True),
        lax.all_gather(down_bias, ("batch", "seq"), axis=0, tiled=True),
    )
    grad_down = left_dot(active_low, grad_branch)
    grad_down_shift = column_total(grad_branch)
    grad_active = right_dot(grad_branch, down_weight)
    gelu_value, gelu_pull = jax.vjp(gelu_exact, upward)
    grad_up_low = gelu_pull(grad_active)[0].astype(jnp.bfloat16)
    grad_up = left_dot(normed_two_low, grad_up_low)
    grad_up_shift = column_total(grad_up_low)
    grad_normed_two = right_dot(grad_up_low, up_weight)
    norm_value, norm_pull = jax.vjp(
        norm_rows, hidden, gain_two.astype(jnp.float32), bias_two.astype(jnp.float32)
    )
    grad_hidden_norm, grad_gain_two, grad_bias_two = norm_pull(grad_normed_two)
    grad_hidden = grad_out + grad_hidden_norm
    mlp_grads = (
        lax.psum_scatter(grad_gain_two, ("batch", "seq"), scatter_dimension=0, tiled=True),
        lax.psum_scatter(grad_bias_two, ("batch", "seq"), scatter_dimension=0, tiled=True),
        lax.psum_scatter(grad_up, ("batch", "seq"), scatter_dimension=0, tiled=True),
        lax.psum_scatter(grad_up_shift, ("batch", "seq"), scatter_dimension=0, tiled=True),
        lax.psum_scatter(grad_down, ("batch", "seq"), scatter_dimension=0, tiled=True),
        lax.psum_scatter(grad_down_shift, ("batch", "seq"), scatter_dimension=0, tiled=True),
    )
    gain_one, bias_one, qkv_weight, query_bias, value_bias, out_weight, out_shift = (
        lax.all_gather(ln1_gain, ("batch", "seq"), axis=0, tiled=True),
        lax.all_gather(ln1_bias, ("batch", "seq"), axis=0, tiled=True),
        lax.all_gather(w_qkv, ("batch", "seq"), axis=0, tiled=True),
        lax.all_gather(q_bias, ("batch", "seq"), axis=0, tiled=True),
        lax.all_gather(v_bias, ("batch", "seq"), axis=0, tiled=True),
        lax.all_gather(w_out, ("batch", "seq"), axis=0, tiled=True),
        lax.all_gather(out_bias, ("batch", "seq"), axis=0, tiled=True),
    )
    gain_one_f = gain_one.astype(jnp.float32)
    bias_one_f = bias_one.astype(jnp.float32)
    grad_hidden_low = grad_hidden.astype(jnp.bfloat16)
    grad_out_weight = left_dot(mixed_low, grad_hidden_low)
    grad_out_shift = column_total(grad_hidden_low)
    grad_mixed = (
        right_dot(grad_hidden_low, out_weight)
        .astype(jnp.bfloat16)
        .reshape(items, own_len, heads, HEAD)
    )
    probs = jnp.exp(score_of() - log_total)
    probs_low = probs.astype(jnp.bfloat16)
    grad_probs = jnp.einsum(
        "nqhe,nkhe->nhqk", grad_mixed, values_all, preferred_element_type=jnp.float32
    )
    grad_scores = probs * (grad_probs - jnp.sum(probs * grad_probs, axis=-1, keepdims=True))
    grad_scores_low = grad_scores.astype(jnp.bfloat16)
    grad_query = (
        jnp.einsum("nhqk,nkhe->nqhe", grad_scores_low, keys_all, preferred_element_type=jnp.float32)
        * scale
    )
    zero_low = jnp.zeros((), jnp.bfloat16)
    live_grads = jnp.where(live_pairs[None, None], grad_scores_low, zero_low)
    live_probs = jnp.where(live_pairs[None, None], probs_low, zero_low)
    grad_keys = (
        jnp.einsum("nhqk,nqhe->nkhe", live_grads, query_items, preferred_element_type=jnp.float32)
        * scale
    )
    grad_values = jnp.einsum(
        "nhqk,nqhe->nkhe", live_probs, grad_mixed, preferred_element_type=jnp.float32
    )

    def split_keys(grads):
        own_part = grads[:, :own_len].reshape(count_rows, width)
        early_part = grads[:, own_len : 2 * own_len].reshape(count_rows, width)
        summ_part = grads[:, 2 * own_len :].reshape(items * summ_len, width)
        return (own_part, early_part, summ_part)

    key_grad_own, key_grad_early, key_grad_summ = split_keys(grad_keys)
    value_grad_own, value_grad_early, value_grad_summ = split_keys(grad_values)
    back_key, back_value = (
        passed_along(key_grad_early.astype(jnp.bfloat16), "seq", -1).astype(key_grad_early.dtype),
        passed_along(value_grad_early.astype(jnp.bfloat16), "seq", -1).astype(
            value_grad_early.dtype
        ),
    )
    summ_key, summ_value = (
        lax.psum(key_grad_summ.astype(jnp.bfloat16), "seq").astype(jnp.float32),
        lax.psum(value_grad_summ.astype(jnp.bfloat16), "seq").astype(jnp.float32),
    )
    is_owner = (seq_index == lax.axis_size("seq") - 1).astype(jnp.float32)

    def add_summary(grads, extra):
        shaped = grads.reshape(items, slots, half, width)
        shaped = shaped.at[:, :, summary_start:].add(
            extra.reshape(items, slots, NSUM, width) * is_owner
        )
        return shaped.reshape(count_rows, width)

    grad_key = add_summary(key_grad_own + back_key, summ_key)
    grad_value = add_summary(value_grad_own + back_value, summ_value)
    grad_merged = jnp.concatenate(
        [grad_query.reshape(count_rows, width), grad_key, grad_value], axis=1
    ).astype(jnp.bfloat16)
    grad_qkv = left_dot(normed_low, grad_merged)
    grad_query_bias = column_total(grad_merged[:, :width])
    grad_value_bias = column_total(grad_merged[:, 2 * width :])
    grad_normed = right_dot(grad_merged, qkv_weight)
    first_value, first_pull = jax.vjp(norm_rows, token_rows, gain_one_f, bias_one_f)
    grad_token_norm, grad_gain_one, grad_bias_one = first_pull(grad_normed)
    grad_tokens = (grad_hidden + grad_token_norm).astype(jnp.bfloat16).reshape(tokens.shape)
    attn_grads = (
        lax.psum_scatter(grad_gain_one, ("batch", "seq"), scatter_dimension=0, tiled=True),
        lax.psum_scatter(grad_bias_one, ("batch", "seq"), scatter_dimension=0, tiled=True),
        lax.psum_scatter(grad_qkv, ("batch", "seq"), scatter_dimension=0, tiled=True),
        lax.psum_scatter(grad_query_bias, ("batch", "seq"), scatter_dimension=0, tiled=True),
        lax.psum_scatter(grad_value_bias, ("batch", "seq"), scatter_dimension=0, tiled=True),
        lax.psum_scatter(grad_out_weight, ("batch", "seq"), scatter_dimension=0, tiled=True),
        lax.psum_scatter(grad_out_shift, ("batch", "seq"), scatter_dimension=0, tiled=True),
    )
    return (block_out, grad_tokens) + tuple(attn_grads) + tuple(mlp_grads)


def solution(mesh):
    return jax.shard_map(
        shards,
        mesh=mesh,
        in_specs=(
            P("batch", None, "seq", None),
            P("batch"),
            P(("batch", "seq")),
            P(("batch", "seq")),
            P(("batch", "seq"), None),
            P(("batch", "seq")),
            P(("batch", "seq")),
            P(("batch", "seq"), None),
            P(("batch", "seq")),
            P(("batch", "seq")),
            P(("batch", "seq")),
            P(("batch", "seq"), None),
            P(("batch", "seq")),
            P(("batch", "seq"), None),
            P(("batch", "seq")),
            P("batch", None, "seq", None),
        ),
        out_specs=(
            P("batch", None, "seq", None),
            P("batch", None, "seq", None),
            P(("batch", "seq")),
            P(("batch", "seq")),
            P(("batch", "seq"), None),
            P(("batch", "seq")),
            P(("batch", "seq")),
            P(("batch", "seq"), None),
            P(("batch", "seq")),
            P(("batch", "seq")),
            P(("batch", "seq")),
            P(("batch", "seq"), None),
            P(("batch", "seq")),
            P(("batch", "seq"), None),
            P(("batch", "seq")),
        ),
        check_vma=False,
    )
```

profile of v0, /device:TPU:1, one launch (start us, length us, event | category | flops | bytes accessed | tf_op | source)
XLA Modules:
  0.0 2531.8 jit_solution(4236400131706761390)
XLA Ops:
  18.7 69.3 %all-reduce.26 = (bf16[768]{0:T(1024)(128)(2,1)S(1)}, bf16[768]{0:T(1024)(128)(2,1)S(1)}, bf16[768]{0:T(1024)(128)(2,1)S(1)}, bf16[768]{0:T(1024)(128)(2,1)S(1)}...) all-reduce(bf16[768]{0:T(1024)(128)(2,1)S(1)} %dynamic-update-slice, ...), channel_id=1, replica_groups=mesh['batch'=64,'seq'=2] {'batch','seq'}, use_global_device_ids=true, to_apply=%add.2 | all-reduce | flops 9216 | bytes 36864
  89.8 231.9 %all-gather.10.cloned.1.call-done = bf16[128,6,2304]{2,1,0:T(8,128)(2,1)} async-done(((bf16[1,6,2304]{2,1,0:T(8,128)(2,1)}), bf16[128,6,2304]{2,1,0:T(8,128)(2,1)}) %all-gather.10.cloned.1.call-update) | async-done | bytes 3538960 | tf_op jit(solution)/shard_map/all_gather | solution.py:85
  321.7 5.0 reshape.527
  342.4 277.9 %all-gather.12.cloned.1.call-done = bf16[128,6,768]{2,1,0:T(8,128)(2,1)} async-done(((bf16[1,6,768]{2,1,0:T(8,128)(2,1)}), bf16[128,6,768]{2,1,0:T(8,128)(2,1)}) %all-gather.12.cloned.1.call-update) | async-done | bytes 1179664 | tf_op jit(solution)/shard_map/all_gather | solution.py:88
  625.3 29.4 %all-reduce.35.cloned.1.call-done = (bf16[1,64,12,64]{1,3,2,0:T(8,128)(2,1)}, bf16[1,64,12,64]{1,3,2,0:T(8,128)(2,1)}) async-done(((bf16[1,64,12,64]{1,3,2,0:T(8,128)(2,1)}, bf16[1,64,12,64]{1,3,2,0:T(8,128)(2,1)}), (bf16[1,64,12,64]{1,3,2,0:T(8,128)(2,1)}, bf16[1,64,12,64]{1,3,2,0:T(8,128)(2,1)})) %all-reduce.35.cloned.1.call-update) | async-done | bytes 196624 | tf_op jit(solution)/shard_map/psum | solution.py:22
  660.3 309.1 %all-gather.14.cloned.1.call-done = bf16[128,6,3072]{2,1,0:T(8,128)(2,1)} async-done(((bf16[1,6,3072]{2,1,0:T(8,128)(2,1)}), bf16[128,6,3072]{2,1,0:T(8,128)(2,1)}) %all-gather.14.cloned.1.call-update) | async-done | bytes 4718608 | tf_op jit(solution)/shard_map/all_gather | solution.py:156
  969.4 7.9 reshape.531
  977.3 4.4 convolution_add_fusion.1
  981.7 298.3 %all-gather.8.cloned.1.call-done = bf16[3072,768]{1,0:T(8,128)(2,1)} async-done(((bf16[24,768]{1,0:T(8,128)(2,1)}), bf16[3072,768]{1,0:T(8,128)(2,1)}) %all-gather.8.cloned.1.call-update) | async-done | bytes 4718608 | tf_op jit(solution)/shard_map/all_gather | solution.py:158
  1280.0 8.1 convert_reduce_fusion
  1306.0 6.0 fusion.54
  1323.0 8.6 collective-permute-start.3
  1336.5 5.1 fusion.42
  1347.3 4.0 fusion.26
  1351.3 744.5 %fusion.44 = (f32[8,2304]{1,0:T(8,128)}, f32[8,768]{1,0:T(8,128)}, f32[8,3072]{1,0:T(8,128)}) fusion(f32[768,2304]{1,0:T(8,128)} %fusion.26, f32[768,768]{1,0:T(8,128)S(1)} %fusion.53, f32[768,3072]{1,0:T(8,128)} %fusion.42), kind=kCustom, calls=%all-reduce-scatter.3 | all-reduce-scatter fusion | flops 6291457 | bytes 19070976
  2097.7 5.8 collective-permute-start.65
  2107.5 3.9 collective-permute-start.64
  2125.1 3.2 collective-permute-start.58
  2128.4 4.0 collective-permute-start.57
  2154.3 3.5 collective-permute-start.46
  2157.8 3.3 collective-permute-start.45
  2166.8 4.6 collective-permute-start.42
  2175.3 4.3 collective-permute-start.39
  2179.6 3.7 collective-permute-start.38
  2199.2 5.2 collective-permute-start.31
  2210.4 6.1 collective-permute-start.26
  2227.1 7.4 collective-permute-start.21
  2249.3 3.4 collective-permute-start.14
  2252.7 4.8 collective-permute-start.13
  2258.9 3.8 fusion.16
  2262.8 3.4 collective-permute-start.11
  2266.2 4.0 collective-permute-start.10
  2275.3 3.3 collective-permute-start.7
  2278.9 4.8 collective-permute-start.6
  2314.6 4.1 collective-permute-start.87
  2325.4 3.2 collective-permute-start.82
  2328.7 5.1 collective-permute-start.81
  2342.1 62.8 %all-reduce.25 = (f32[768]{0:T(1024)S(1)}, f32[768]{0:T(1024)S(1)}, f32[768]{0:T(1024)S(1)}, f32[768]{0:T(1024)S(1)}, f32[768]{0:T(1024)S(1)}, /*index=5*/f32[76...) all-reduce(f32[768]{0:T(1024)S(1)} %get-tuple-element.41, ...), channel_id=2, replica_groups=mesh['batch'=64,'seq'=2] {'batch','seq'}, use_global_device_ids=true, to_apply=%region_16.17.clone | all-reduce | flops 9216 | bytes 73728
  2410.4 8.6 concatenate.34
  2419.1 4.1 collective-permute-start.77
  2423.2 4.2 collective-permute-start.76
  2427.4 4.0 collective-permute-start.75
  2431.4 4.6 collective-permute-start.74
  2436.0 3.2 collective-permute-start.73
  2440.0 32.6 %concatenate.33 = f32[262,2304]{1,0:T(8,128)S(1)} concatenate(f32[6,2304]{1,0:T(8,128)} %copy-done.74, f32[8,2304]{1,0:T(8,128)} %copy-done.71, f32[8,2304]{1,0:T(8,128)} %copy-done.72, f32[8,2304]{1,0:T(8,128)} %copy-done.73, f32[8,2304]{1,0:T(8,128)} %copy-done.75, f32[8,2304]{1,0:T(8,128)} %copy-done.76, f32[8,2304]{1,0:T(8,128)} %copy-done.77, f32[8,2304]{1,0:T(8,128)} %copy-done.78, ...), dimensions={0} | concatenate | bytes 4829184
  2474.3 5.3 collective-permute-start.71
  2479.6 3.8 collective-permute-start.70
  2492.4 31.5 %concatenate.35 = f32[262,3072]{1,0:T(8,128)S(1)} concatenate(f32[6,3072]{1,0:T(8,128)S(1)} %collective-permute-done.99, f32[8,3072]{1,0:T(8,128)S(1)} %collective-permute-done.98, f32[8,3072]{1,0:T(8,128)} %copy-done.46, f32[8,3072]{1,0:T(8,128)} %copy-done.47, f32[8,3072]{1,0:T(8,128)} %copy-done.48, f32[8,3072]{1,0:T(8,128)} %copy-done.49, f32[8,3072]{1,0:T(8,128)} %copy-done.50, ...), dimensions={0} | concatenate | bytes 6438912
  (684 shorter events, 243.3 us)
Async XLA Ops:
  7.2 314.5 %all-gather.10.cloned.1.call-start = ((), (), s32[]{:S(2)}) async-start(), calls=%async_computation.3 | async-start | bytes 4755456 | tf_op jit(solution)/shard_map/all_gather | solution.py:85
  7.9 612.3 %all-gather.12.cloned.1.call-start = ((), (), s32[]{:S(2)}) async-start(), calls=%async_computation.4 | async-start | bytes 1585152 | tf_op jit(solution)/shard_map/all_gather | solution.py:88
  8.7 646.1 %all-reduce.35.cloned.1.call-start = ((), (), s32[]{:S(2)}) async-start(), calls=%async_computation.7 | async-start | bytes 786432 | tf_op jit(solution)/shard_map/psum | solution.py:22
  333.1 636.2 %all-gather.14.cloned.1.call-start = ((), (), s32[]{:S(2)}) async-start(), calls=%async_computation.5 | async-start | bytes 6340608 | tf_op jit(solution)/shard_map/all_gather | solution.py:156
  333.7 946.2 %all-gather.8.cloned.1.call-start = ((), (), s32[]{:S(2)}) async-start(), calls=%async_computation.1 | async-start | bytes 4755456 | tf_op jit(solution)/shard_map/all_gather | solution.py:158
  334.3 1007.3 %all-reduce.33.cloned.1.call-start = ((), (), s32[]{:S(2)}) async-start(), calls=%async_computation.6 | async-start | bytes 393216 | tf_op jit(solution)/shard_map/psum | solution.py:260
  337.9 286.5 %collective-permute-start = (bf16[128,768]{1,0:T(8,128)(2,1)S(1)}, bf16[128,768]{1,0:T(8,128)(2,1)S(1)}, u32[]{:S(2)}, u32[]{:S(2)}) collective-permute-start(bf16[128,768]{1,0:T(8,128)(2,1)S(1)} %copy-done.21), channel_id=1, source_target_pairs={{0,1},{2,3},{4,5},{6,7},{8,9},{10,11},{12,13},{14,15},{16,17},{18,... | collective-permute-start | bytes 589832 | tf_op jit(solution)/shard_map/ppermute | solution.py:17
  340.2 284.9 %collective-permute-start.1 = (bf16[128,768]{1,0:T(8,128)(2,1)S(1)}, bf16[128,768]{1,0:T(8,128)(2,1)S(1)}, u32[]{:S(2)}, u32[]{:S(2)}) collective-permute-start(bf16[128,768]{1,0:T(8,128)(2,1)S(1)} %copy-done.19), channel_id=1, source_target_pairs={{0,1},{2,3},{4,5},{6,7},{8,9},{10,11},{12,13},{14,15},{16,17},{18,... | collective-permute-start | bytes 589832 | tf_op jit(solution)/shard_map/ppermute | solution.py:17
  1305.9 1218.6 %reduce-scatter.8.cloned.1.call-start = ((), (), s32[]{:S(2)}) async-start(), calls=%async_computation.2 | async-start | bytes 9510912 | tf_op jit(solution)/shard_map/reduce_scatter | solution.py:200
  1323.0 22.3 collective-permute-start.3
  2095.7 20.1 collective-permute-start.66
  2097.7 21.3 collective-permute-start.65
  2115.9 16.6 collective-permute-start.61
  2119.0 15.7 collective-permute-start.60
  2154.3 17.1 collective-permute-start.46
  2157.8 16.1 collective-permute-start.45
  2164.2 15.4 collective-permute-start.43
  2166.8 16.5 collective-permute-start.42
  2183.4 22.3 collective-permute-start.34
  2184.7 22.8 collective-permute-start.33
  2186.1 22.8 collective-permute-start.32
  2210.4 16.7 collective-permute-start.26
  2216.5 17.9 collective-permute-start.25
  2219.4 17.6 collective-permute-start.24
  2220.9 17.4 collective-permute-start.23
  2223.8 16.1 collective-permute-start.22
  2227.1 16.6 collective-permute-start.21
  2239.9 17.6 collective-permute-start.17
  2243.6 19.1 collective-permute-start.16
  2246.2 19.9 collective-permute-start.15
  2249.3 20.9 collective-permute-start.14
  2252.7 20.3 collective-permute-start.13
  2257.6 17.8 collective-permute-start.12
  2262.8 16.1 collective-permute-start.11
  2266.2 17.5 collective-permute-start.10
  2270.2 16.0 collective-permute-start.9
  2273.1 15.6 collective-permute-start.8
  2325.4 93.6 %collective-permute-start.82 = (f32[8,3072]{1,0:T(8,128)S(1)}, f32[8,3072]{1,0:T(8,128)S(1)}, u32[]{:S(2)}, u32[]{:S(2)}) collective-permute-start(f32[8,3072]{1,0:T(8,128)S(1)} %copy-done.22), channel_id=1, source_target_pairs={{0,15},{1,16},{2,17},{3,18},{4,19},{5,20},{6,21},{7,22},{8,23},{9,... | collective-permute-start | bytes 294920
  2328.7 94.5 %collective-permute-start.81 = (f32[8,3072]{1,0:T(8,128)S(1)}, f32[8,3072]{1,0:T(8,128)S(1)}, u32[]{:S(2)}, u32[]{:S(2)}) collective-permute-start(f32[8,3072]{1,0:T(8,128)S(1)} %copy-done.22), channel_id=1, source_target_pairs={{0,14},{1,15},{2,16},{3,17},{4,18},{5,19},{6,20},{7,21},{8,22},{9,... | collective-permute-start | bytes 294920
  2333.9 93.6 %collective-permute-start.80 = (f32[8,3072]{1,0:T(8,128)S(1)}, f32[8,3072]{1,0:T(8,128)S(1)}, u32[]{:S(2)}, u32[]{:S(2)}) collective-permute-start(f32[8,3072]{1,0:T(8,128)S(1)} %copy-done.22), channel_id=1, source_target_pairs={{0,13},{1,14},{2,15},{3,16},{4,17},{5,18},{6,19},{7,20},{8,21},{9,... | collective-permute-start | bytes 294920
  2335.2 96.2 %collective-permute-start.79 = (f32[8,3072]{1,0:T(8,128)S(1)}, f32[8,3072]{1,0:T(8,128)S(1)}, u32[]{:S(2)}, u32[]{:S(2)}) collective-permute-start(f32[8,3072]{1,0:T(8,128)S(1)} %copy-done.22), channel_id=1, source_target_pairs={{0,12},{1,13},{2,14},{3,15},{4,16},{5,17},{6,18},{7,19},{8,20},{9,... | collective-permute-start | bytes 294920
  2337.7 98.3 %collective-permute-start.78 = (f32[8,3072]{1,0:T(8,128)S(1)}, f32[8,3072]{1,0:T(8,128)S(1)}, u32[]{:S(2)}, u32[]{:S(2)}) collective-permute-start(f32[8,3072]{1,0:T(8,128)S(1)} %copy-done.22), channel_id=1, source_target_pairs={{0,11},{1,12},{2,13},{3,14},{4,15},{5,16},{6,17},{7,18},{8,19},{9,... | collective-permute-start | bytes 294920
  2419.1 53.5 %collective-permute-start.77 = (f32[8,3072]{1,0:T(8,128)S(1)}, f32[8,3072]{1,0:T(8,128)S(1)}, u32[]{:S(2)}, u32[]{:S(2)}) collective-permute-start(f32[8,3072]{1,0:T(8,128)S(1)} %copy-done.22), channel_id=1, source_target_pairs={{0,10},{1,11},{2,12},{3,13},{4,14},{5,15},{6,16},{7,17},{8,18},{9,... | collective-permute-start | bytes 294920
  2423.2 51.0 %collective-permute-start.76 = (f32[8,3072]{1,0:T(8,128)S(1)}, f32[8,3072]{1,0:T(8,128)}, u32[]{:S(2)}, u32[]{:S(2)}) collective-permute-start(f32[8,3072]{1,0:T(8,128)S(1)} %copy-done.22), channel_id=1, source_target_pairs={{0,9},{1,10},{2,11},{3,12},{4,13},{5,14},{6,15},{7,16},{8,17},{9,1... | collective-permute-start | bytes 294920
  2427.4 52.1 %collective-permute-start.75 = (f32[8,3072]{1,0:T(8,128)S(1)}, f32[8,3072]{1,0:T(8,128)}, u32[]{:S(2)}, u32[]{:S(2)}) collective-permute-start(f32[8,3072]{1,0:T(8,128)S(1)} %copy-done.22), channel_id=1, source_target_pairs={{0,8},{1,9},{2,10},{3,11},{4,12},{5,13},{6,14},{7,15},{8,16},{9,17... | collective-permute-start | bytes 294920
  2431.4 52.0 %collective-permute-start.74 = (f32[8,3072]{1,0:T(8,128)S(1)}, f32[8,3072]{1,0:T(8,128)}, u32[]{:S(2)}, u32[]{:S(2)}) collective-permute-start(f32[8,3072]{1,0:T(8,128)S(1)} %copy-done.22), channel_id=1, source_target_pairs={{0,7},{1,8},{2,9},{3,10},{4,11},{5,12},{6,13},{7,14},{8,15},{9,16}... | collective-permute-start | bytes 294920
  2436.0 50.1 %collective-permute-start.73 = (f32[8,3072]{1,0:T(8,128)S(1)}, f32[8,3072]{1,0:T(8,128)}, u32[]{:S(2)}, u32[]{:S(2)}) collective-permute-start(f32[8,3072]{1,0:T(8,128)S(1)} %copy-done.22), channel_id=1, source_target_pairs={{0,6},{1,7},{2,8},{3,9},{4,10},{5,11},{6,12},{7,13},{8,14},{9,15},... | collective-permute-start | bytes 294920
  2472.6 16.7 collective-permute-start.72
  (245 other events, 11955.8 us)
Sparse Core Ops, SparseCore 0:
  9.7 311.9 all-gather.9
  323.4 296.8 all-gather.11
  622.7 31.9 all-reduce.34
  656.4 312.9 all-gather.13
  971.0 308.9 all-gather.7
  1306.0 30.2 all-reduce.32
  1339.4 652.9 reduce-scatter.7
where the time goes:
time: 2550 us; the launch traced here: 2530 us
  waiting for transfers between devices  1160 us (45%)
  blocking collectives  877 us (34%)
  starting transfers between devices  279 us (11%)
  local copies, waits for them, and re-layouts  133 us (5%)
  matrix products  48.6 us (2%)
    unnamed x3, blocking collectives  877 us
    all_gather x1, waiting for transfers between devices, shards(): lax.all_gather(w_up, ('batch', 'seq'), axis=0, tiled=True)  309 us
    all_gather x1, waiting for transfers between devices, shards(): lax.all_gather(w_down, ('batch', 'seq'), axis=0, tiled=True)  298 us
    all_gather x1, waiting for transfers between devices, shards(): lax.all_gather(w_out, ('batch', 'seq'), axis=0, tiled=True)  278 us
    unnamed x96, starting transfers between devices  264 us
    all_gather x1, waiting for transfers between devices, shards(): lax.all_gather(w_qkv, ('batch', 'seq'), axis=0, tiled=True)  232 us
    unnamed x412, local copies, waits for them, and re-layouts  112 us
  transfers between devices with their start and end apart: 107, of which 9 were waited for; matrix products, arithmetic and copies ran while one was open for 36% of the time, Pallas kernels for 0%

commit v1 on v0

v1 whole, which is shorter than its diff:
```python
import jax
import jax.numpy as jnp
import numpy as np
from jax import lax
from jax.experimental import pallas as pl
from jax.experimental.pallas import tpu as pltpu
from jax.sharding import Mesh
from jax.sharding import PartitionSpec as P

WIDTH = 768
HEAD = 64
NSUM = 16
SLOTS = 4
SEGLEN = 64
HALFSEG = 32
FF = 3072

EPSILON = 1e-05
MASKED = -1e30
SCALE = HEAD ** (-0.5)

AXES = ("x", "yh", "z", "c", "yl")
SIZES = (4, 2, 4, 2, 2)
QUAD_AXES = ("x", "yh", "z")
QUADS = 32
DEVICES = 128
ROWS = 256
OWN = 128
HALF = WIDTH // 2
QKV = 3 * HALF
UP = FF // 2
SMALL = 128
VMEM_LIMIT = 60 * 1024 * 1024

F32 = jnp.float32
BF16 = jnp.bfloat16


def dot_nn(left, right):
    return jnp.dot(left, right, preferred_element_type=F32)


def dot_tn(left, right):
    return lax.dot_general(left, right, (((0,), (0,)), ((), ())), preferred_element_type=F32)


def dot_nt(left, right):
    return lax.dot_general(left, right, (((1,), (1,)), ((), ())), preferred_element_type=F32)


def normalised(values):
    center = values - jnp.mean(values, axis=-1, keepdims=True)
    spread = jnp.mean(center * center, axis=-1, keepdims=True)
    scale = lax.rsqrt(spread + EPSILON)
    return center * scale, scale


def norm_back(grad, unit, scale, gain):
    inner = grad * gain
    mean = jnp.mean(inner, axis=-1, keepdims=True)
    along = jnp.mean(inner * unit, axis=-1, keepdims=True)
    return scale * (inner - mean - unit * along)


def total(values):
    return jnp.sum(values.astype(F32), axis=0, keepdims=True)


def swap_halves(values):
    return jnp.concatenate([values[OWN:], values[:OWN]], axis=0)


def masks(core):
    def place(dim):
        row = lax.broadcasted_iota(jnp.int32, (ROWS, ROWS), dim)
        second = (row >= OWN).astype(jnp.int32)
        inner = row - second * OWN
        half = core + second - 2 * core * second
        slot = inner // HALFSEG
        return slot, half * HALFSEG + inner - slot * HALFSEG

    query_slot, query_pos = place(0)
    key_slot, key_pos = place(1)
    same = (query_slot == key_slot) & (key_pos <= query_pos)
    earlier = (key_slot < query_slot) & (key_pos >= SEGLEN - NSUM)
    return same | earlier, key_slot >= query_slot - 2


def head_lanes(j):
    lane = lax.broadcasted_iota(jnp.int32, (1, 2 * HEAD), 1)
    return jnp.where(lane // HEAD == j, 1.0, 0.0).astype(BF16)


def attend_kernel(core_ref, x_ref, gain_ref, shift_ref, w_ref, b_ref, a_ref, qkv_ref, o_ref, lse_ref):
    unit, _ = normalised(x_ref[...].astype(F32))
    a = (unit * gain_ref[...] + shift_ref[...]).astype(BF16)
    a_ref[...] = a
    qkv_ref[...] = (dot_nn(a, w_ref[...]) + b_ref[...]).astype(BF16)
    admitted, _ = masks(core_ref[0])
    lane = lax.broadcasted_iota(jnp.int32, (ROWS, 128), 1)
    kept = jnp.zeros((ROWS, 128), F32)
    for pair in range(3):
        lanes = pl.ds(128 * pair, 128)
        query = qkv_ref[:, lanes]
        key = qkv_ref[:, pl.ds(HALF + 128 * pair, 128)]
        value = qkv_ref[:, pl.ds(2 * HALF + 128 * pair, 128)]
        out = jnp.zeros((ROWS, 128), F32)
        for j in range(2):
            only = head_lanes(j)
            scores = jnp.where(admitted, dot_nt(query * only, key) * SCALE, MASKED)
            top = jnp.max(scores, axis=-1, keepdims=True)
            grown = jnp.exp(scores - top)
            amount = jnp.sum(grown, axis=-1, keepdims=True)
            kept = jnp.where(lane == 2 * pair + j, top + jnp.log(amount), kept)
            probs = (grown * (1.0 / amount)).astype(BF16)
            out += dot_nn(probs, value * only)
        o_ref[:, lanes] = out.astype(BF16)
    lse_ref[...] = kept


def mlp_kernel(
    core_ref, x_ref, own_o_ref, far_o_ref, own_out_ref, far_out_ref, vec_ref, up_ref, up_b_ref, down_ref, g_ref,
    h_ref, m_own_ref, m_far_ref, grad_a_ref, grad_up_ref, grad_down_ref, grad_up_b_ref, grad_down_b_ref,
):
    core = core_ref[0]
    here = pl.multiple_of(core * HALF, 128)
    there = pl.multiple_of((1 - core) * HALF, 128)
    own_o = own_o_ref[...]
    far_o = swap_halves(far_o_ref[...])
    for out_ref, at in ((own_out_ref, here), (far_out_ref, there)):
        part = dot_nn(own_o, out_ref[pl.ds(here, HALF), :]) + dot_nn(far_o, out_ref[pl.ds(there, HALF), :])
        h_ref[:, pl.ds(at, HALF)] = part
    hidden = x_ref[...].astype(F32) + (h_ref[...] + vec_ref[0:1, :])
    h_ref[...] = hidden
    unit, _ = normalised(hidden)
    a = (unit * vec_ref[1:2, :] + vec_ref[2:3, :]).astype(BF16)
    g = g_ref[...]
    branch = jnp.zeros((ROWS, WIDTH), F32)
    grad_a = jnp.zeros((ROWS, WIDTH), F32)
    step = 512
    for i in range(UP // step):
        cols = pl.ds(i * step, step)
        up = up_ref[:, cols]
        down = down_ref[cols, :]
        u = dot_nn(a, up) + up_b_ref[:, cols]
        phi = 0.5 * (1.0 + lax.erf(u * (0.5**0.5)))
        z = (u * phi).astype(BF16)
        slope = phi + u * (jnp.exp(-0.5 * u * u) * (2.0 * jnp.pi) ** (-0.5))
        branch += dot_nn(z, down)
        gu = (dot_nt(g, down) * slope).astype(BF16)
        grad_down_ref[cols, :] = dot_tn(z, g).astype(BF16)
        grad_up_ref[:, cols] = dot_tn(a, gu).astype(BF16)
        grad_up_b_ref[:, cols] = total(gu)
        grad_a += dot_nt(gu, up)
    m_own_ref[...] = branch[:OWN] + hidden[:OWN] + vec_ref[3:4, :]
    m_far_ref[...] = branch[OWN:]
    grad_a_ref[...] = grad_a
    grad_down_b_ref[...] = total(g[:OWN])


def back_kernel(
    core_ref, h_ref, g_ref, own_grad_ref, far_grad_ref, vec_ref, own_o_ref, far_o_ref, own_out_ref, far_out_ref,
    qkv_ref, lse_ref, a_ref, w_ref,
    grad_w_ref, grad_out_ref, own_x_ref, far_x_ref, gh_ref, vec_out_ref, grad_b_ref,
    gh_low_ref, go_ref, gqkv_ref,
):
    core = core_ref[0]
    here = pl.multiple_of(core * HALF, 128)
    there = pl.multiple_of((1 - core) * HALF, 128)
    grad_a = own_grad_ref[...] + swap_halves(far_grad_ref[...])
    unit, scale = normalised(h_ref[...])
    grad_h = g_ref[...].astype(F32) + norm_back(grad_a, unit, scale, vec_ref[1:2, :])
    gh_ref[...] = grad_h[:OWN]
    low = grad_h.astype(BF16)
    gh_low_ref[...] = low
    vec_out_ref[0:1, :] = total(low[:OWN])
    vec_out_ref[1:2, :] = total(grad_a[:OWN] * unit[:OWN])
    vec_out_ref[2:3, :] = total(grad_a[:OWN])
    low_here = gh_low_ref[:, pl.ds(here, HALF)]
    low_there = gh_low_ref[:, pl.ds(there, HALF)]
    own_o = own_o_ref[...]
    far_o = swap_halves(far_o_ref[...])
    grad_out_ref[pl.ds(here, HALF), :] = dot_tn(own_o, low_here).astype(BF16)
    grad_out_ref[pl.ds(there, HALF), :] = dot_tn(far_o, low_here).astype(BF16)
    rows = pl.ds(here, HALF)
    go_ref[...] = (dot_nt(low_here, own_out_ref[rows, :]) + dot_nt(low_there, far_out_ref[rows, :])).astype(BF16)
    admitted, live = masks(core)
    live = jnp.where(live, 1.0, 0.0)
    lane = lax.broadcasted_iota(jnp.int32, (ROWS, 128), 1)
    for pair in range(3):
        query = qkv_ref[:, pl.ds(128 * pair, 128)]
        key = qkv_ref[:, pl.ds(HALF + 128 * pair, 128)]
        value = qkv_ref[:, pl.ds(2 * HALF + 128 * pair, 128)]
        go = go_ref[:, pl.ds(128 * pair, 128)]
        gq = jnp.zeros((ROWS, 128), F32)
        gk = jnp.zeros((ROWS, 128), F32)
        gv = jnp.zeros((ROWS, 128), F32)
        for j in range(2):
            only = head_lanes(j)
            lse = jnp.sum(jnp.where(lane == 2 * pair + j, lse_ref[...], 0.0), axis=-1, keepdims=True)
            scores = jnp.where(admitted, dot_nt(query * only, key) * SCALE, MASKED)
            probs = jnp.exp(scores - lse)
            grad_p = dot_nt(go * only, value)
            grad_s = probs * (grad_p - jnp.sum(probs * grad_p, axis=-1, keepdims=True))
            gq += dot_nn(grad_s.astype(BF16), key * only)
            gk += dot_tn((grad_s * live).astype(BF16), query * only)
            gv += dot_tn((probs * live).astype(BF16), go * only)
        gqkv_ref[:, pl.ds(128 * pair, 128)] = (gq * SCALE).astype(BF16)
        gqkv_ref[:, pl.ds(HALF + 128 * pair, 128)] = (gk * SCALE).astype(BF16)
        gqkv_ref[:, pl.ds(2 * HALF + 128 * pair, 128)] = gv.astype(BF16)
    gqkv = gqkv_ref[...]
    grad_w_ref[...] = dot_tn(a_ref[...], gqkv).astype(BF16)
    grad_b_ref[...] = total(gqkv)
    grad_x = dot_nt(gqkv, w_ref[...])
    own_x_ref[...] = grad_x[:OWN]
    far_x_ref[...] = grad_x[OWN:]


def tokens_kernel(x_ref, own_ref, far_ref, gh_ref, gain_ref, out_ref, vec_ref):
    grad = own_ref[...] + far_ref[...]
    unit, scale = normalised(x_ref[...].astype(F32))
    out_ref[...] = (gh_ref[...] + norm_back(grad, unit, scale, gain_ref[...])).astype(BF16)
    vec_ref[0:1, :] = total(grad * unit)
    vec_ref[1:2, :] = total(grad)


def call(kernel, core, args, outs, scratch=()):
    specs = [pl.BlockSpec(memory_space=pltpu.VMEM)] * len(args)
    if core is not None:
        args = (core,) + tuple(args)
        specs = [pl.BlockSpec(memory_space=pltpu.SMEM)] + specs
    return pl.pallas_call(
        kernel,
        out_shape=tuple(jax.ShapeDtypeStruct(s, d) for s, d in outs),
        in_specs=specs,
        out_specs=tuple(pl.BlockSpec(memory_space=pltpu.VMEM) for _ in outs),
        scratch_shapes=[pltpu.VMEM(s, d) for s, d in scratch],
        compiler_params=pltpu.CompilerParams(vmem_limit_bytes=VMEM_LIMIT),
    )(*args)


def between_cores(values):
    return lax.ppermute(values, "c", [(0, 1), (1, 0)])


def between_chips(values):
    return lax.ppermute(values, "yl", [(0, 1), (1, 0)])


def swap_items(values):
    return lax.ppermute(values, ("c", "yl"), [(0, 0), (1, 2), (2, 1), (3, 3)])


HALVES = [(64 * c + 2 * k + yl, 4 * k + 2 * c + yl) for k in range(QUADS) for c in range(2) for yl in range(2)]


def halves_out(values):
    return lax.ppermute(values, AXES, HALVES)


def halves_back(values):
    return lax.ppermute(values, AXES, [(b, a) for a, b in HALVES])


def gather(block):
    spread = jnp.broadcast_to(block[None], (QUADS,) + block.shape)
    got = lax.all_to_all(spread, QUAD_AXES, 0, 0, tiled=True)
    return got.reshape(QUADS * block.shape[0], block.shape[1])


def reduce(grads):
    rows = grads.shape[0] // QUADS
    got = lax.all_to_all(grads.reshape(QUADS, rows, grads.shape[1]), QUAD_AXES, 0, 0, tiled=True)
    return jnp.sum(got.astype(F32), axis=0)


def by_place(place, first, second, axis=0):
    return jnp.where(
        place == 0, jnp.concatenate([first, second], axis), jnp.concatenate([second, first], axis)
    )


def shards(
    tokens,
    segment_counts,
    ln1_gain,
    ln1_bias,
    w_qkv,
    q_bias,
    v_bias,
    w_out,
    out_bias,
    ln2_gain,
    ln2_bias,
    w_up,
    up_bias,
    w_down,
    down_bias,
    cotangent,
):
    core = lax.axis_index("c")
    side = lax.axis_index("yl")
    core_arg = core.astype(jnp.int32).reshape(1)
    present = jnp.arange(SLOTS) < segment_counts[0]
    present_rows = jnp.repeat(present, HALFSEG)[:, None]
    cot = jnp.where(present_rows, cotangent.reshape(OWN, WIDTH), 0).astype(BF16)
    mine = swap_items(jnp.concatenate([tokens.reshape(OWN, WIDTH), cot], axis=1))
    item = jnp.concatenate([mine, between_cores(mine)], axis=0)
    x, g = item[:, :WIDTH], item[:, WIDTH:]

    small = jnp.stack([ln1_gain, ln1_bias, q_bias, v_bias, out_bias, ln2_gain, ln2_bias, down_bias], axis=1)
    small = jnp.concatenate([small, up_bias.reshape(6, 4), jnp.zeros((6, SMALL - 12), BF16)], axis=1)

    def half_of(t):
        parts = [w_qkv[:, j * WIDTH + t * HALF : j * WIDTH + (t + 1) * HALF] for j in range(3)]
        parts += [small, w_out[:, t * HALF : (t + 1) * HALF], w_up[:, t * UP : (t + 1) * UP]]
        return jnp.concatenate(parts, axis=1)

    first, second = half_of(0), half_of(1)
    rows = lax.all_to_all(jnp.stack([first, first, second, second]), ("c", "yl"), 0, 0, tiled=True)
    rows = rows.reshape(24, QKV + SMALL + HALF + UP)
    near = halves_out(w_down)
    down_rows = by_place(side, near, between_chips(near))

    attn = gather(rows[:, : QKV + SMALL + HALF])
    w_in = attn[:, :QKV]
    small_all = attn[:, QKV : QKV + SMALL]
    own_out = attn[:, QKV + SMALL :]
    far_out = between_cores(own_out)
    vectors = small_all[:, :12].T.astype(F32)
    at = core * HALF
    query_b = lax.dynamic_slice(vectors[2:3], (0, at), (1, HALF))
    value_b = lax.dynamic_slice(vectors[3:4], (0, at), (1, HALF))
    qkv_b = jnp.concatenate([query_b, jnp.zeros_like(query_b), value_b], axis=1)
    up_b = lax.dynamic_slice(small_all, (at, 8), (HALF, 4)).reshape(1, UP).astype(F32)
    mid_vec = jnp.concatenate([vectors[4:8], jnp.zeros((4, WIDTH), F32)], axis=0)

    a1, qkv, own_o, lse = call(
        attend_kernel,
        core_arg,
        (x, vectors[0:1], vectors[1:2], w_in, qkv_b),
        (((ROWS, WIDTH), BF16), ((ROWS, QKV), BF16), ((ROWS, HALF), BF16), ((ROWS, 128), F32)),
    )
    far_o = between_cores(own_o)
    w_up_all = gather(rows[:, QKV + SMALL + HALF :])
    w_down_all = gather(down_rows)
    hidden, m_own, m_far, grad_a_own, grad_up, grad_down, grad_up_b, grad_down_b = call(
        mlp_kernel,
        core_arg,
        (x, own_o, far_o, own_out, far_out, mid_vec, w_up_all, up_b, w_down_all, g),
        (
            ((ROWS, WIDTH), F32),
            ((OWN, WIDTH), F32),
            ((OWN, WIDTH), F32),
            ((ROWS, WIDTH), F32),
            ((WIDTH, UP), BF16),
            ((UP, WIDTH), BF16),
            ((1, UP), F32),
            ((1, WIDTH), F32),
        ),
    )
    grad_a_far = between_cores(grad_a_own)
    block = swap_items((m_own + between_cores(m_far)).astype(BF16))
    block_out = jnp.where(present_rows, block, 0).reshape(tokens.shape)

    grad_w, grad_out, own_x, far_x, gh, vec_mid, grad_b = call(
        back_kernel,
        core_arg,
        (hidden, g, grad_a_own, grad_a_far, mid_vec, own_o, far_o, own_out, far_out, qkv, lse, a1, w_in),
        (
            ((WIDTH, QKV), BF16),
            ((WIDTH, HALF), BF16),
            ((OWN, WIDTH), F32),
            ((OWN, WIDTH), F32),
            ((OWN, WIDTH), F32),
            ((3, WIDTH), F32),
            ((1, QKV), F32),
        ),
        (((ROWS, WIDTH), BF16), ((ROWS, HALF), BF16), ((ROWS, QKV), BF16)),
    )
    grad_x, vec_first = call(
        tokens_kernel,
        None,
        (x[:OWN], own_x, between_cores(far_x), gh, vectors[0:1]),
        (((OWN, WIDTH), BF16), ((2, WIDTH), F32)),
    )
    grad_tokens = swap_items(grad_x).reshape(tokens.shape)

    def placed(values, length):
        return lax.dynamic_update_slice(jnp.zeros((1, length), F32), values, (0, core * values.shape[1]))

    grad_vec = jnp.concatenate(
        [
            vec_first,
            placed(grad_b[:, :HALF], WIDTH),
            placed(grad_b[:, 2 * HALF :], WIDTH),
            vec_mid,
            grad_down_b,
            placed(grad_up_b, FF).reshape(WIDTH, 4).T,
        ],
        axis=0,
    ).T
    high = grad_vec.astype(BF16)
    low = (grad_vec - high.astype(F32)).astype(BF16)
    grad_small = jnp.concatenate([high, low, jnp.zeros((WIDTH, SMALL - 24), BF16)], axis=1)

    down_sum = reduce(grad_down)
    down_near = jnp.where(side == 0, down_sum[:24], down_sum[24:])
    down_other = jnp.where(side == 0, down_sum[24:], down_sum[:24])
    out_down = halves_back(down_near + between_chips(down_other))
    row_sum = jnp.concatenate(
        [reduce(jnp.concatenate([grad_w, grad_small, grad_out], axis=1)), reduce(grad_up)], axis=1
    )
    got = lax.all_to_all(row_sum.reshape(4, 6, row_sum.shape[1]), ("c", "yl"), 0, 0, tiled=True)
    both = got[0::2] + got[1::2]
    out_qkv = jnp.concatenate(
        [both[t, :, j * HALF : (j + 1) * HALF] for j in range(3) for t in range(2)], axis=1
    )
    vec = both[0, :, QKV : QKV + SMALL] + both[1, :, QKV : QKV + SMALL]
    vec = vec[:, :12] + vec[:, 12:24]
    out_out = jnp.concatenate([both[t, :, QKV + SMALL : QKV + SMALL + HALF] for t in range(2)], axis=1)
    out_up = jnp.concatenate([both[t, :, QKV + SMALL + HALF :] for t in range(2)], axis=1)
    return (
        block_out,
        grad_tokens,
        vec[:, 0],
        vec[:, 1],
        out_qkv,
        vec[:, 2],
        vec[:, 3],
        out_out,
        vec[:, 4],
        vec[:, 5],
        vec[:, 6],
        out_up,
        vec[:, 8:12].reshape(24),
        out_down,
        vec[:, 7],
    )


def solution(mesh):
    torus = Mesh(np.asarray(mesh.devices).reshape(SIZES), AXES)
    items = P(("x", "yh", "z", "c"), None, "yl", None)
    part, rows = P(AXES), P(AXES, None)
    return jax.shard_map(
        shards,
        mesh=torus,
        in_specs=(
            items, P(("x", "yh", "z", "c")), part, part, rows, part, part, rows, part, part, part, rows, part, rows,
            part, items,
        ),
        out_specs=(
            items, items, part, part, rows, part, part, rows, part, part, part, rows, part, rows, part,
        ),
        check_vma=False,
    )
```

time: 2550 us -> 308 us (0.12)
  waiting for transfers between devices: 1160 us -> 112 us
  blocking collectives: 877 us -> 39.7 us
  starting transfers between devices: 279 us -> 67.9 us
  local copies, waits for them, and re-layouts: 133 us -> 46.9 us
  matrix products: 48.6 us -> 0 us
  Pallas kernels: 0 us -> 25.7 us
    all_gather x4 -> x0, waiting for transfers between devices: 1120 us -> none  [the longest x1 309 us: shards(): lax.all_gather(w_up, ('batch', 'seq'), axis=0, tiled=True)]
    unnamed x3 -> x0, blocking collectives: 877 us -> none
    unnamed x96 -> x0, starting transfers between devices: 264 us -> none
    unnamed x412 -> x31, local copies, waits for them, and re-layouts: 112 us -> 5.03 us
    all_to_all x0 -> x7, waiting for transfers between devices: none -> 84.6 us  [the longest x3 74.4 us: gather(): got = lax.all_to_all(spread, QUAD_AXES, 0, 0, tiled=True)]
    dot_general x18 -> x0, matrix products: 48.6 us -> none  [the longest x4 16.5 us: left_dot(): lax.dot_general(left, right, (((0,), (0,)), ((), ())), preferred_element_...]
    all_to_all x0 -> x7, starting transfers between devices: none -> 45.9 us  [the longest x3 25.1 us: gather(): got = lax.all_to_all(spread, QUAD_AXES, 0, 0, tiled=True)]
    all_to_all x0 -> x1, blocking collectives: none -> 39.7 us  [reduce(): lax.all_to_all(grads.reshape(QUADS, rows, grads.shape[1]), QUAD_AXES, 0,...]
  transfers between devices with their start and end apart: 107 -> 20, of which waited for: 9 -> 8; matrix products, arithmetic and copies ran while one was open for 36% -> 15% of each run, Pallas kernels for 0% -> 5%
where the time goes in v1:
time: 308 us; the launch traced here: 303 us
  waiting for transfers between devices  112 us (36%)
  starting transfers between devices  67.9 us (22%)
  local copies, waits for them, and re-layouts  46.9 us (15%)
  blocking collectives  39.7 us (13%)
  Pallas kernels  25.7 us (8%)
  other arithmetic  8.96 us (3%)
    all_to_all x3, waiting for transfers between devices, gather(): got = lax.all_to_all(spread, QUAD_AXES, 0, 0, tiled=True)  74.4 us
    all_to_all x1, blocking collectives, reduce(): lax.all_to_all(grads.reshape(QUADS, rows, grads.shape[1]), QUAD_AXES, 0,...  39.7 us
    pallas_call x4, Pallas kernels, call(): pl.pallas_call(kernel, out_shape=tuple((jax.ShapeDtypeStruct(s, d) for s,...  25.7 us
    all_to_all x3, starting transfers between devices, gather(): got = lax.all_to_all(spread, QUAD_AXES, 0, 0, tiled=True)  25.1 us
    ppermute x2, waiting for transfers between devices, between_chips(): return lax.ppermute(values, 'yl', [(0, 1), (1, 0)])  25.1 us
    all_to_all x2, starting transfers between devices, reduce(): lax.all_to_all(grads.reshape(QUADS, rows, grads.shape[1]), QUAD_AXES, 0,...  13.9 us
    ppermute x3, starting transfers between devices, swap_items(): return lax.ppermute(values, ('c', 'yl'), [(0, 0), (1, 2), (2, 1), (3, 3)])  8.37 us
    all_to_all x1, waiting for transfers between devices, shards(): lax.all_to_all(row_sum.reshape(4, 6, row_sum.shape[1]), ('c', 'yl'), 0, 0...  6.68 us
  transfers between devices with their start and end apart: 20, of which 8 were waited for; matrix products, arithmetic and copies ran while one was open for 15% of the time, Pallas kernels for 5%

profile of v1, /device:TPU:1, one launch (start us, length us, event | category | flops | bytes accessed | tf_op | source)
XLA Modules:
  0.0 303.2 jit_solution(4658402785452433808)
XLA Ops:
  0.6 4.9 %collective-permute-start.4 = (bf16[24,768]{1,0:T(8,128)(2,1)}, bf16[24,768]{1,0:T(8,128)(2,1)S(1)}, u32[]{:S(2)}, u32[]{:S(2)}) collective-permute-start(bf16[24,768]{1,0:T(8,128)(2,1)} %param.29), channel_id=1, source_target_pairs={{0,0},{1,1},{64,2},{65,3},{2,4},{3,5},{66,6},{67,7},{4,8},{5,9},{6... | collective-permute-start | bytes 110600 | tf_op jit(solution)/shard_map/ppermute | solution.py:258
  6.3 0.8 fusion.6
  14.1 1.4 collective-permute-start.5
  16.2 3.4 %all-to-all-start = ((bf16[4,6,3200]{2,1,0:T(8,128)(2,1)}), bf16[4,6,3200]{2,1,0:T(8,128)(2,1)S(1)}, u32[]{:S(2)}, u32[]{:S(2)}) async-start(bf16[4,6,3200]{2,1,0:T(8,128)(2,1)} %pad_maximum_fusion.2), calls=%async_computation | async-start | bytes 409600 | tf_op jit(solution)/shard_map/all_to_all | solution.py:320
  19.7 3.5 %all-to-all-done = bf16[4,6,3200]{2,1,0:T(8,128)(2,1)S(1)} async-done(((bf16[4,6,3200]{2,1,0:T(8,128)(2,1)}), bf16[4,6,3200]{2,1,0:T(8,128)(2,1)S(1)}, u32[]{:S(2)}, u32[]{:S(2)}) %all-to-all-start) | async-done | bytes 153632 | tf_op jit(solution)/shard_map/all_to_all | solution.py:320
  23.2 1.6 broadcast_in_dim.60
  24.7 10.5 %all-to-all-start.3 = ((bf16[32,48,768]{2,1,0:T(8,128)(2,1)}), bf16[32,48,768]{2,1,0:T(8,128)(2,1)S(1)}, u32[]{:S(2)}, u32[]{:S(2)}) async-start(bf16[32,48,768]{2,1,0:T(8,128)(2,1)} %broadcast_in_dim.60), calls=%async_computation.3 | async-start | bytes 4718592 | tf_op jit(solution)/shard_map/all_to_all | solution.py:267
  35.3 30.5 %all-to-all-done.3 = bf16[32,48,768]{2,1,0:T(8,128)(2,1)S(1)} async-done(((bf16[32,48,768]{2,1,0:T(8,128)(2,1)}), bf16[32,48,768]{2,1,0:T(8,128)(2,1)S(1)}, u32[]{:S(2)}, u32[]{:S(2)}) %all-to-all-start.3) | async-done | bytes 2359328 | tf_op jit(solution)/shard_map/all_to_all | solution.py:267
  65.8 1.8 broadcast_in_dim.57
  68.0 7.8 %all-to-all-start.1 = ((bf16[32,24,1664]{2,1,0:T(8,128)(2,1)}), bf16[32,24,1664]{2,1,0:T(8,128)(2,1)S(1)}, u32[]{:S(2)}, u32[]{:S(2)}) async-start(bf16[32,24,1664]{2,1,0:T(8,128)(2,1)} %broadcast_in_dim.57), calls=%async_computation.1 | async-start | bytes 5111808 | tf_op jit(solution)/shard_map/all_to_all | solution.py:267
  76.7 2.8 collective-permute-start
  80.2 29.5 %all-to-all-done.1 = bf16[32,24,1664]{2,1,0:T(8,128)(2,1)S(1)} async-done(((bf16[32,24,1664]{2,1,0:T(8,128)(2,1)}), bf16[32,24,1664]{2,1,0:T(8,128)(2,1)S(1)}, u32[]{:S(2)}, u32[]{:S(2)}) %all-to-all-start.1) | async-done | bytes 2555936 | tf_op jit(solution)/shard_map/all_to_all | solution.py:267
  109.6 2.5 broadcast_in_dim.59
  112.1 6.9 %all-to-all-start.2 = ((bf16[32,24,1536]{2,1,0:T(8,128)(2,1)}), bf16[32,24,1536]{2,1,0:T(8,128)(2,1)}, u32[]{:S(2)}, u32[]{:S(2)}) async-start(bf16[32,24,1536]{2,1,0:T(8,128)(2,1)} %broadcast_in_dim.59), calls=%async_computation.2 | async-start | bytes 4718592 | tf_op jit(solution)/shard_map/all_to_all | solution.py:267
  119.0 1.4 collective-permute-start.1
  120.5 1.3 collective-permute-done.1
  121.8 0.9 fusion.3
  123.4 1.4 slice.223.w_ref
  125.0 1.9 copy.144
  129.2 4.3 %shard_map.271 = (bf16[256,768]{1,0:T(8,128)(2,1)}, bf16[256,1152]{1,0:T(8,128)(2,1)}, bf16[256,384]{1,0:T(8,128)(2,1)}, f32[256,128]{1,0:T(8,128)}) custom-call(s32[1]{0:T(128)} %bitcast.1.core_ref, bf16[256,768]{1,0:T(8,128)(2,1)} %get-tuple-element.68.x_ref, f32[1,768]{1,0:T(1,128)} %get-tuple-element.76.gain_ref, f32[1,768]{1,0:T(1,128)} %get-tuple-element.75.shift_ref, ...), custom_call_target="tpu_custom_call" | custom-call | tf_op jit(solution)/shard_map/pallas_call | solution.py:232
  135.1 14.4 %all-to-all-done.2 = bf16[32,24,1536]{2,1,0:T(8,128)(2,1)} async-done(((bf16[32,24,1536]{2,1,0:T(8,128)(2,1)}), bf16[32,24,1536]{2,1,0:T(8,128)(2,1)}, u32[]{:S(2)}, u32[]{:S(2)}) %all-to-all-start.2) | async-done | bytes 2359328 | tf_op jit(solution)/shard_map/all_to_all | solution.py:267
  149.6 10.5 %shard_map.272 = (f32[256,768]{1,0:T(8,128)}, f32[128,768]{1,0:T(8,128)}, f32[128,768]{1,0:T(8,128)}, f32[256,768]{1,0:T(8,128)}, bf16[768,1536]{1,0:T(8,128)(2,...) custom-call(s32[1]{0:T(128)} %bitcast.1.core_ref, bf16[256,768]{1,0:T(8,128)(2,1)} %get-tuple-element.68.x_ref, ...), custom_call_target="tpu_custom_call" | custom-call | tf_op jit(solution)/shard_map/pallas_call | solution.py:232
  160.1 39.7 %all_to_all.40 = bf16[32,48,768]{2,1,0:T(8,128)(2,1)} all-to-all(bf16[32,48,768]{2,1,0:T(8,128)(2,1)} %bitcast.73), channel_id=1, replica_groups=mesh['x'=4,'yh'=2,'z'=4,'c'=2,'yl'=2] {'x','yh','z'}, dimensions={0} | all-to-all | bytes 4718592 | tf_op jit(solution)/shard_map/all_to_all | solution.py:273
  199.8 4.4 %all-to-all-start.5 = ((bf16[32,24,1536]{2,1,0:T(8,128)(2,1)}), bf16[32,24,1536]{2,1,0:T(8,128)(2,1)S(1)}, u32[]{:S(2)}, u32[]{:S(2)}) async-start(bf16[32,24,1536]{2,1,0:T(8,128)(2,1)} %bitcast.72), calls=%async_computation.5 | async-start | bytes 4718592 | tf_op jit(solution)/shard_map/all_to_all | solution.py:273
  204.2 2.5 collective-permute-start.8
  209.2 8.5 %shard_map.273 = (bf16[768,1152]{1,0:T(8,128)(2,1)}, bf16[768,384]{1,0:T(8,128)(2,1)}, f32[128,768]{1,0:T(8,128)}, f32[128,768]{1,0:T(8,128)}, f32[128,768]{1,0:...) custom-call(s32[1]{0:T(128)} %bitcast.1.core_ref, f32[256,768]{1,0:T(8,128)} %get-tuple-element.39.h_ref, ...), custom_call_target="tpu_custom_call" | custom-call | tf_op jit(solution)/shard_map/pallas_call | solution.py:232
  218.5 0.8 copy.139
  219.3 0.8 copy.140
  220.2 0.9 copy.142
  221.1 0.8 broadcast.11.clone
  221.9 1.6 constant_dynamic-update-slice_fusion.10
  223.5 0.8 broadcast.11.clone.1
  224.3 1.6 constant_dynamic-update-slice_fusion.9
  226.0 2.3 shard_map.274
  228.3 1.7 copy.141
  230.0 2.4 concatenate.61
  232.4 1.0 fusion
  233.5 5.1 %concatenate.62 = bf16[768,1664]{1,0:T(8,128)(2,1)} concatenate(bf16[768,1152]{1,0:T(8,128)(2,1)} %get-tuple-element.48, bf16[768,12]{1,0:T(8,128)(2,1)S(1)} %get-tuple-element.66, bf16[768,12]{1,0:T(8,128)(2,1)S(1)} %get-tuple-element.65, bf16[768,104]{1,0:T(8,128)(2,1)S(1)} %broadcast_in_dim.62, bf16[768,384]{1,0:T(8,128)(2,1)} %get-tuple-element.54), dimensions={1} | concatenate | bytes 5111808 | tf_op jit(solution)/shard_map/concatenate | solution.py:412
  238.6 1.4 copy-done.1
  240.0 9.5 %all-to-all-start.4 = ((bf16[32,24,1664]{2,1,0:T(8,128)(2,1)}), bf16[32,24,1664]{2,1,0:T(8,128)(2,1)S(1)}, u32[]{:S(2)}, u32[]{:S(2)}) async-start(bf16[32,24,1664]{2,1,0:T(8,128)(2,1)} %bitcast.22), calls=%async_computation.4 | async-start | bytes 5111808 | tf_op jit(solution)/shard_map/all_to_all | solution.py:273
  250.3 1.3 collective-permute-done.6
  251.7 1.9 collective-permute-start.7
  253.6 3.6 %collective-permute-start.10 = (bf16[128,768]{1,0:T(8,128)(2,1)}, bf16[128,768]{1,0:T(8,128)(2,1)S(1)}, u32[]{:S(2)}, u32[]{:S(2)}) collective-permute-start(bf16[128,768]{1,0:T(8,128)(2,1)} %get-tuple-element.47), channel_id=1, source_target_pairs={{0,0},{1,2},{2,1},{3,3},{4,4},{5,6},{6,5},{7,7},{8,8},{9,10},{10,9... | collective-permute-start | bytes 589832 | tf_op jit(solution)/shard_map/ppermute | solution.py:251
  257.3 2.0 convert_reduce_fusion.1
  259.7 25.1 %collective-permute-done.11 = f32[24,768]{1,0:T(8,128)S(1)} collective-permute-done((f32[24,768]{1,0:T(8,128)S(1)}, f32[24,768]{1,0:T(8,128)S(1)}, u32[]{:S(2)}, u32[]{:S(2)}) %collective-permute-start.11) | collective-permute-done | bytes 73760 | tf_op jit(solution)/shard_map/ppermute | solution.py:247
  284.8 1.9 collective-permute-start.12
  287.9 3.6 %all-to-all-start.6 = ((f32[4,6,3200]{2,1,0:T(8,128)}), f32[4,6,3200]{2,1,0:T(8,128)S(1)}, u32[]{:S(2)}, u32[]{:S(2)}) async-start(f32[4,6,3200]{2,1,0:T(8,128)} %reshape.139), calls=%async_computation.6 | async-start | bytes 819200 | tf_op jit(solution)/shard_map/all_to_all | solution.py:414
  292.3 6.7 %all-to-all-done.6 = f32[4,6,3200]{2,1,0:T(8,128)S(1)} async-done(((f32[4,6,3200]{2,1,0:T(8,128)}), f32[4,6,3200]{2,1,0:T(8,128)S(1)}, u32[]{:S(2)}, u32[]{:S(2)}) %all-to-all-start.6) | async-done | bytes 307232 | tf_op jit(solution)/shard_map/all_to_all | solution.py:414
  (112 shorter events, 25.3 us)
Async XLA Ops:
  0.6 13.5 %collective-permute-start.4 = (bf16[24,768]{1,0:T(8,128)(2,1)}, bf16[24,768]{1,0:T(8,128)(2,1)S(1)}, u32[]{:S(2)}, u32[]{:S(2)}) collective-permute-start(bf16[24,768]{1,0:T(8,128)(2,1)} %param.29), channel_id=1, source_target_pairs={{0,0},{1,1},{64,2},{65,3},{2,4},{3,5},{66,6},{67,7},{4,8},{5,9},{6... | collective-permute-start | bytes 110600 | tf_op jit(solution)/shard_map/ppermute | solution.py:258
  14.1 5.5 %collective-permute-start.5 = (bf16[24,768]{1,0:T(8,128)(2,1)S(1)}, bf16[24,768]{1,0:T(8,128)(2,1)S(1)}, u32[]{:S(2)}, u32[]{:S(2)}) collective-permute-start(bf16[24,768]{1,0:T(8,128)(2,1)S(1)} %collective-permute-done.4), channel_id=1, source_target_pairs={{0,1},{1,0},{2,3},{3,2},{4,5},{5,4},{6,7},{7,6},{8,9},{9,8},{10,11... | collective-permute-start | bytes 110600 | tf_op jit(solution)/shard_map/ppermute | solution.py:247
  16.2 6.9 %all-to-all-start = ((bf16[4,6,3200]{2,1,0:T(8,128)(2,1)}), bf16[4,6,3200]{2,1,0:T(8,128)(2,1)S(1)}, u32[]{:S(2)}, u32[]{:S(2)}) async-start(bf16[4,6,3200]{2,1,0:T(8,128)(2,1)} %pad_maximum_fusion.2), calls=%async_computation | async-start | bytes 409600 | tf_op jit(solution)/shard_map/all_to_all | solution.py:320
  24.7 41.1 %all-to-all-start.3 = ((bf16[32,48,768]{2,1,0:T(8,128)(2,1)}), bf16[32,48,768]{2,1,0:T(8,128)(2,1)S(1)}, u32[]{:S(2)}, u32[]{:S(2)}) async-start(bf16[32,48,768]{2,1,0:T(8,128)(2,1)} %broadcast_in_dim.60), calls=%async_computation.3 | async-start | bytes 4718592 | tf_op jit(solution)/shard_map/all_to_all | solution.py:267
  65.8 2.2 copy-start
  67.6 9.0 %copy-start.5 = (bf16[1,4,32,768]{3,2,1,0:T(8,128)(2,1)S(1)}, bf16[1,4,32,768]{3,2,1,0:T(8,128)(2,1)}, u32[]{:S(2)}) copy-start(bf16[1,4,32,768]{3,2,1,0:T(8,128)(2,1)} %param.31) | copy-start | bytes 589828
  67.6 9.1 %copy-start.6 = (bf16[1,4,32,768]{3,2,1,0:T(8,128)(2,1)S(1)}, bf16[1,4,32,768]{3,2,1,0:T(8,128)(2,1)}, u32[]{:S(2)}) copy-start(bf16[1,4,32,768]{3,2,1,0:T(8,128)(2,1)} %param.16) | copy-start | bytes 589828
  68.0 41.6 %all-to-all-start.1 = ((bf16[32,24,1664]{2,1,0:T(8,128)(2,1)}), bf16[32,24,1664]{2,1,0:T(8,128)(2,1)S(1)}, u32[]{:S(2)}, u32[]{:S(2)}) async-start(bf16[32,24,1664]{2,1,0:T(8,128)(2,1)} %broadcast_in_dim.57), calls=%async_computation.1 | async-start | bytes 5111808 | tf_op jit(solution)/shard_map/all_to_all | solution.py:267
  76.7 42.3 %collective-permute-start = (bf16[128,1536]{1,0:T(8,128)(2,1)S(1)}, bf16[128,1536]{1,0:T(8,128)(2,1)S(1)}, u32[]{:S(2)}, u32[]{:S(2)}) collective-permute-start(bf16[128,1536]{1,0:T(8,128)(2,1)S(1)} %pad_maximum_fusion), channel_id=1, source_target_pairs={{0,0},{1,2},{2,1},{3,3},{4,4},{5,6},{6,5},{7,7},{8,8},{9,10},{10,9... | collective-permute-start | bytes 1179656 | tf_op jit(solution)/shard_map/ppermute | solution.py:251
  112.1 37.5 %all-to-all-start.2 = ((bf16[32,24,1536]{2,1,0:T(8,128)(2,1)}), bf16[32,24,1536]{2,1,0:T(8,128)(2,1)}, u32[]{:S(2)}, u32[]{:S(2)}) async-start(bf16[32,24,1536]{2,1,0:T(8,128)(2,1)} %broadcast_in_dim.59), calls=%async_computation.2 | async-start | bytes 4718592 | tf_op jit(solution)/shard_map/all_to_all | solution.py:267
  119.0 2.8 collective-permute-start.1
  125.0 24.6 %copy-start.3 = (bf16[768,384]{1,0:T(8,128)(2,1)}, bf16[768,384]{1,0:T(8,128)(2,1)S(1)}, u32[]{:S(2)}) copy-start(bf16[768,384]{1,0:T(8,128)(2,1)S(1)} %slice.226.own_out_ref) | copy-start | bytes 1769476
  126.8 22.7 %collective-permute-start.3 = (bf16[768,384]{1,0:T(8,128)(2,1)S(1)}, bf16[768,384]{1,0:T(8,128)(2,1)}, u32[]{:S(2)}, u32[]{:S(2)}) collective-permute-start(bf16[768,384]{1,0:T(8,128)(2,1)S(1)} %slice.226.own_out_ref), channel_id=1, source_target_pairs={{0,2},{2,0},{1,3},{3,1},{4,6},{6,4},{5,7},{7,5},{8,10},{10,8},{9,1... | collective-permute-start | bytes 1769480 | tf_op jit(solution)/shard_map/ppermute | solution.py:243
  133.5 16.1 %collective-permute-start.2 = (bf16[256,384]{1,0:T(8,128)(2,1)}, bf16[256,384]{1,0:T(8,128)(2,1)}, u32[]{:S(2)}, u32[]{:S(2)}) collective-permute-start(bf16[256,384]{1,0:T(8,128)(2,1)} %get-tuple-element.36.own_o_ref), channel_id=1, source_target_pairs={{0,2},{2,0},{1,3},{3,1},{4,6},{6,4},{5,7},{7,5},{8,10},{10,8},{9,1... | collective-permute-start | bytes 589832 | tf_op jit(solution)/shard_map/ppermute | solution.py:243
  199.8 7.5 %copy-start.7 = (f32[1,1536]{1,0:T(1,128)S(1)}, f32[1,1536]{1,0:T(1,128)}, u32[]{:S(2)}) copy-start(f32[1,1536]{1,0:T(1,128)} %get-tuple-element.53) | copy-start | bytes 18436
  199.8 9.2 %copy-start.8 = (f32[1,768]{1,0:T(1,128)S(1)}, f32[1,768]{1,0:T(1,128)}, u32[]{:S(2)}) copy-start(f32[1,768]{1,0:T(1,128)} %get-tuple-element.52) | copy-start | bytes 9220
  199.8 38.8 %all-to-all-start.5 = ((bf16[32,24,1536]{2,1,0:T(8,128)(2,1)}), bf16[32,24,1536]{2,1,0:T(8,128)(2,1)S(1)}, u32[]{:S(2)}, u32[]{:S(2)}) async-start(bf16[32,24,1536]{2,1,0:T(8,128)(2,1)} %bitcast.72), calls=%async_computation.5 | async-start | bytes 4718592 | tf_op jit(solution)/shard_map/all_to_all | solution.py:273
  204.2 5.0 %collective-permute-start.8 = (f32[256,768]{1,0:T(8,128)}, f32[256,768]{1,0:T(8,128)}, u32[]{:S(2)}, u32[]{:S(2)}) collective-permute-start(f32[256,768]{1,0:T(8,128)} %get-tuple-element.40.own_grad_ref), channel_id=1, source_target_pairs={{0,2},{2,0},{1,3},{3,1},{4,6},{6,4},{5,7},{7,5},{8,10},{10,8},{9,1... | collective-permute-start | bytes 2359304 | tf_op jit(solution)/shard_map/ppermute | solution.py:243
  217.7 8.3 %collective-permute-start.9 = (f32[128,768]{1,0:T(8,128)}, f32[128,768]{1,0:T(8,128)}, u32[]{:S(2)}, u32[]{:S(2)}) collective-permute-start(f32[128,768]{1,0:T(8,128)} %get-tuple-element.45), channel_id=1, source_target_pairs={{0,2},{2,0},{1,3},{3,1},{4,6},{6,4},{5,7},{7,5},{8,10},{10,8},{9,1... | collective-permute-start | bytes 1179656 | tf_op jit(solution)/shard_map/ppermute | solution.py:243
  238.6 1.4 copy-start.1
  238.6 10.9 %copy-start.10 = (f32[128,768]{1,0:T(8,128)S(1)}, f32[128,768]{1,0:T(8,128)}, u32[]{:S(2)}) copy-start(f32[128,768]{1,0:T(8,128)} %get-tuple-element.38) | copy-start | bytes 1179652
  238.6 13.1 %copy-start.4 = (f32[128,768]{1,0:T(8,128)S(1)}, f32[128,768]{1,0:T(8,128)}, u32[]{:S(2)}) copy-start(f32[128,768]{1,0:T(8,128)} %get-tuple-element.37) | copy-start | bytes 1179652
  240.0 46.7 %all-to-all-start.4 = ((bf16[32,24,1664]{2,1,0:T(8,128)(2,1)}), bf16[32,24,1664]{2,1,0:T(8,128)(2,1)S(1)}, u32[]{:S(2)}, u32[]{:S(2)}) async-start(bf16[32,24,1664]{2,1,0:T(8,128)(2,1)} %bitcast.22), calls=%async_computation.4 | async-start | bytes 5111808 | tf_op jit(solution)/shard_map/all_to_all | solution.py:273
  249.5 9.9 %copy-start.2 = (bf16[32,24,1536]{2,1,0:T(8,128)(2,1)S(1)}, bf16[32,24,1536]{2,1,0:T(8,128)(2,1)}, u32[]{:S(2)}) copy-start(bf16[32,24,1536]{2,1,0:T(8,128)(2,1)} %copy-done.1) | copy-start | bytes 7077892
  249.6 2.1 collective-permute-start.6
  251.7 39.8 %collective-permute-start.7 = (bf16[128,768]{1,0:T(8,128)(2,1)S(1)}, bf16[128,768]{1,0:T(8,128)(2,1)S(1)}, u32[]{:S(2)}, u32[]{:S(2)}) collective-permute-start(bf16[128,768]{1,0:T(8,128)(2,1)S(1)} %add_convert_fusion), channel_id=1, source_target_pairs={{0,0},{1,2},{2,1},{3,3},{4,4},{5,6},{6,5},{7,7},{8,8},{9,10},{10,9... | collective-permute-start | bytes 589832 | tf_op jit(solution)/shard_map/ppermute | solution.py:251
  253.6 38.6 %collective-permute-start.10 = (bf16[128,768]{1,0:T(8,128)(2,1)}, bf16[128,768]{1,0:T(8,128)(2,1)S(1)}, u32[]{:S(2)}, u32[]{:S(2)}) collective-permute-start(bf16[128,768]{1,0:T(8,128)(2,1)} %get-tuple-element.47), channel_id=1, source_target_pairs={{0,0},{1,2},{2,1},{3,3},{4,4},{5,6},{6,5},{7,7},{8,8},{9,10},{10,9... | collective-permute-start | bytes 589832 | tf_op jit(solution)/shard_map/ppermute | solution.py:251
  259.3 25.5 %collective-permute-start.11 = (f32[24,768]{1,0:T(8,128)S(1)}, f32[24,768]{1,0:T(8,128)S(1)}, u32[]{:S(2)}, u32[]{:S(2)}) collective-permute-start(f32[24,768]{1,0:T(8,128)S(1)} %slice_select_fusion), channel_id=1, source_target_pairs={{0,1},{1,0},{2,3},{3,2},{4,5},{5,4},{6,7},{7,6},{8,9},{9,8},{10,11... | collective-permute-start | bytes 221192 | tf_op jit(solution)/shard_map/ppermute | solution.py:247
  284.8 7.5 %collective-permute-start.12 = (f32[24,768]{1,0:T(8,128)S(1)}, f32[24,768]{1,0:T(8,128)S(1)}, u32[]{:S(2)}, u32[]{:S(2)}) collective-permute-start(f32[24,768]{1,0:T(8,128)S(1)} %select_add_fusion), channel_id=1, source_target_pairs={{0,0},{1,1},{2,64},{3,65},{4,2},{5,3},{6,66},{7,67},{8,4},{9,5},{1... | collective-permute-start | bytes 221192 | tf_op jit(solution)/shard_map/ppermute | solution.py:262
  287.9 11.0 %all-to-all-start.6 = ((f32[4,6,3200]{2,1,0:T(8,128)}), f32[4,6,3200]{2,1,0:T(8,128)S(1)}, u32[]{:S(2)}, u32[]{:S(2)}) async-start(f32[4,6,3200]{2,1,0:T(8,128)} %reshape.139), calls=%async_computation.6 | async-start | bytes 819200 | tf_op jit(solution)/shard_map/all_to_all | solution.py:414
  300.0 3.2 %copy-start.9 = (f32[6,2304]{1,0:T(8,128)}, f32[6,2304]{1,0:T(8,128)S(1)}, u32[]{:S(2)}) copy-start(f32[6,2304]{1,0:T(8,128)S(1)} %constant_dynamic-update-slice_fusion.2) | copy-start | bytes 165892

commit v2 on v1

--- a/solution.py
+++ b/solution.py
@@ -30,6 +30,10 @@
 QKV = 3 * HALF
 UP = FF // 2
 SMALL = 128
+ATTN = QKV + SMALL + HALF
+UP_ROWS = WIDTH // 4
+DOWN_ROWS = UP // 4
+RING_Y = ("yh", "yl")
 VMEM_LIMIT = 60 * 1024 * 1024
 
 F32 = jnp.float32
@@ -91,12 +95,12 @@
     return jnp.where(lane // HEAD == j, 1.0, 0.0).astype(BF16)
 
 
-def attend_kernel(core_ref, x_ref, gain_ref, shift_ref, w_ref, b_ref, a_ref, qkv_ref, o_ref, lse_ref):
+def attend_kernel(place_ref, x_ref, gain_ref, shift_ref, w_ref, b_ref, a_ref, qkv_ref, o_ref, lse_ref):
     unit, _ = normalised(x_ref[...].astype(F32))
     a = (unit * gain_ref[...] + shift_ref[...]).astype(BF16)
     a_ref[...] = a
     qkv_ref[...] = (dot_nn(a, w_ref[...]) + b_ref[...]).astype(BF16)
-    admitted, _ = masks(core_ref[0])
+    admitted, _ = masks(place_ref[0])
     lane = lax.broadcasted_iota(jnp.int32, (ROWS, 128), 1)
     kept = jnp.zeros((ROWS, 128), F32)
     for pair in range(3):
@@ -119,10 +123,16 @@
 
 
 def mlp_kernel(
-    core_ref, x_ref, own_o_ref, far_o_ref, own_out_ref, far_out_ref, vec_ref, up_ref, up_b_ref, down_ref, g_ref,
-    h_ref, m_own_ref, m_far_ref, grad_a_ref, grad_up_ref, grad_down_ref, grad_up_b_ref, grad_down_b_ref,
+    place_ref, x_ref, own_o_ref, far_o_ref, own_out_ref, far_out_ref, vec_ref, up_b_ref, g_ref,
+    up_0, up_1, up_2, up_3, down_0, down_1, down_2, down_3,
+    h_ref, m_own_ref, m_far_ref, grad_a_ref, grad_up_b_ref, grad_down_b_ref,
+    gup_0, gup_1, gup_2, gup_3, gdown_0, gdown_1, gdown_2, gdown_3,
+    up_ref, down_ref, grad_up_ref, grad_down_ref,
 ):
-    core = core_ref[0]
+    core, x_at, y_at = place_ref[0], place_ref[1], place_ref[2]
+    for j, (up, down) in enumerate(((up_0, down_0), (up_1, down_1), (up_2, down_2), (up_3, down_3))):
+        up_ref[pl.ds(pl.multiple_of(lax.rem(x_at + j, 4) * UP_ROWS, 64), UP_ROWS), :] = up[...]
+        down_ref[pl.ds(pl.multiple_of(lax.rem(y_at + j, 4) * DOWN_ROWS, 128), DOWN_ROWS), :] = down[...]
     here = pl.multiple_of(core * HALF, 128)
     there = pl.multiple_of((1 - core) * HALF, 128)
     own_o = own_o_ref[...]
@@ -156,15 +166,17 @@
     m_far_ref[...] = branch[OWN:]
     grad_a_ref[...] = grad_a
     grad_down_b_ref[...] = total(g[:OWN])
+    for j, (gup, gdown) in enumerate(((gup_0, gdown_0), (gup_1, gdown_1), (gup_2, gdown_2), (gup_3, gdown_3))):
+        gup[...] = grad_up_ref[pl.ds(pl.multiple_of(lax.rem(x_at + j, 4) * UP_ROWS, 64), UP_ROWS), :]
+        gdown[...] = grad_down_ref[pl.ds(pl.multiple_of(lax.rem(y_at + j, 4) * DOWN_ROWS, 128), DOWN_ROWS), :]
 
 
 def back_kernel(
-    core_ref, h_ref, g_ref, own_grad_ref, far_grad_ref, vec_ref, own_o_ref, far_o_ref, own_out_ref, far_out_ref,
-    qkv_ref, lse_ref, a_ref, w_ref,
-    grad_w_ref, grad_out_ref, own_x_ref, far_x_ref, gh_ref, vec_out_ref, grad_b_ref,
-    gh_low_ref, go_ref, gqkv_ref,
+    place_ref, h_ref, g_ref, own_grad_ref, far_grad_ref, vec_ref, own_out_ref, far_out_ref, qkv_ref, lse_ref, w_ref,
+    gqkv_ref, gh_low_ref, own_x_ref, far_x_ref, gh_ref, vec_out_ref,
+    go_ref,
 ):
-    core = core_ref[0]
+    core = place_ref[0]
     here = pl.multiple_of(core * HALF, 128)
     there = pl.multiple_of((1 - core) * HALF, 128)
     grad_a = own_grad_ref[...] + swap_halves(far_grad_ref[...])
@@ -178,10 +190,6 @@
     vec_out_ref[2:3, :] = total(grad_a[:OWN])
     low_here = gh_low_ref[:, pl.ds(here, HALF)]
     low_there = gh_low_ref[:, pl.ds(there, HALF)]
-    own_o = own_o_ref[...]
-    far_o = swap_halves(far_o_ref[...])
-    grad_out_ref[pl.ds(here, HALF), :] = dot_tn(own_o, low_here).astype(BF16)
-    grad_out_ref[pl.ds(there, HALF), :] = dot_tn(far_o, low_here).astype(BF16)
     rows = pl.ds(here, HALF)
     go_ref[...] = (dot_nt(low_here, own_out_ref[rows, :]) + dot_nt(low_there, far_out_ref[rows, :])).astype(BF16)
     admitted, live = masks(core)
@@ -208,20 +216,42 @@
         gqkv_ref[:, pl.ds(128 * pair, 128)] = (gq * SCALE).astype(BF16)
         gqkv_ref[:, pl.ds(HALF + 128 * pair, 128)] = (gk * SCALE).astype(BF16)
         gqkv_ref[:, pl.ds(2 * HALF + 128 * pair, 128)] = gv.astype(BF16)
-    gqkv = gqkv_ref[...]
-    grad_w_ref[...] = dot_tn(a_ref[...], gqkv).astype(BF16)
-    grad_b_ref[...] = total(gqkv)
-    grad_x = dot_nt(gqkv, w_ref[...])
+    grad_x = dot_nt(gqkv_ref[...], w_ref[...])
     own_x_ref[...] = grad_x[:OWN]
     far_x_ref[...] = grad_x[OWN:]
 
 
-def tokens_kernel(x_ref, own_ref, far_ref, gh_ref, gain_ref, out_ref, vec_ref):
-    grad = own_ref[...] + far_ref[...]
-    unit, scale = normalised(x_ref[...].astype(F32))
+def weights_kernel(
+    place_ref, x_ref, a_ref, gqkv_ref, own_o_ref, far_o_ref, gh_low_ref, own_x_ref, far_x_ref, gh_ref, gain_ref,
+    mid_ref, down_b_ref, up_cols_ref,
+    message_ref, out_ref,
+    rows_ref,
+):
+    core = place_ref[0]
+    here = pl.multiple_of(core * HALF, 128)
+    there = pl.multiple_of((1 - core) * HALF, 128)
+    grad = own_x_ref[...] + far_x_ref[...]
+    unit, scale = normalised(x_ref[:OWN].astype(F32))
     out_ref[...] = (gh_ref[...] + norm_back(grad, unit, scale, gain_ref[...])).astype(BF16)
-    vec_ref[0:1, :] = total(grad * unit)
-    vec_ref[1:2, :] = total(grad)
+    gqkv = gqkv_ref[...]
+    sums = total(gqkv)
+    rows_ref[...] = jnp.zeros((128, WIDTH), F32)
+    rows_ref[0:1, :] = total(grad * unit)
+    rows_ref[1:2, :] = total(grad)
+    rows_ref[2:3, pl.ds(here, HALF)] = sums[:, :HALF]
+    rows_ref[3:4, pl.ds(here, HALF)] = sums[:, 2 * HALF :]
+    rows_ref[4:7, :] = mid_ref[...]
+    rows_ref[7:8, :] = down_b_ref[...]
+    full = rows_ref[0:8, :]
+    high = full.astype(BF16).astype(F32)
+    rows_ref[0:8, :] = high
+    rows_ref[16:24, :] = full - high
+    message_ref[:, pl.ds(QKV, SMALL)] = (rows_ref[...].T + up_cols_ref[...]).astype(BF16)
+    message_ref[:, pl.ds(0, QKV)] = dot_tn(a_ref[...], gqkv).astype(BF16)
+    low_here = gh_low_ref[:, pl.ds(here, HALF)]
+    outs = pl.ds(QKV + SMALL, HALF)
+    message_ref[pl.ds(here, HALF), outs] = dot_tn(own_o_ref[...], low_here).astype(BF16)
+    message_ref[pl.ds(there, HALF), outs] = dot_tn(swap_halves(far_o_ref[...]), low_here).astype(BF16)
 
 
 def call(kernel, core, args, outs, scratch=()):
@@ -251,7 +281,14 @@
     return lax.ppermute(values, ("c", "yl"), [(0, 0), (1, 2), (2, 1), (3, 3)])
 
 
-HALVES = [(64 * c + 2 * k + yl, 4 * k + 2 * c + yl) for k in range(QUADS) for c in range(2) for yl in range(2)]
+HALVES = [
+    (64 * c + 16 * (2 * yh + yl) + 4 * z + x, (((x * 2 + yh) * 4 + z) * 2 + c) * 2 + yl)
+    for x in range(4)
+    for yh in range(2)
+    for z in range(4)
+    for c in range(2)
+    for yl in range(2)
+]
 
 
 def halves_out(values):
@@ -260,6 +297,28 @@
 
 def halves_back(values):
     return lax.ppermute(values, AXES, [(b, a) for a, b in HALVES])
+
+
+def ring(values, axis, by):
+    return lax.ppermute(values, axis, [(i, (i + by) % 4) for i in range(4)])
+
+
+def ring_gather(block, axis):
+    return [block, ring(block, axis, -1), ring(block, axis, 2), ring(block, axis, 1)]
+
+
+def ring_order(blocks, at):
+    return jnp.concatenate([lax.select_n(lax.rem(j - at + 4, 4), *blocks) for j in range(4)], axis=0)
+
+
+def ring_reduce(blocks, axis):
+    got = [ring(blocks[1], axis, 1), ring(blocks[2], axis, 2), ring(blocks[3], axis, -1)]
+    return sum((g.astype(F32) for g in got), blocks[0].astype(F32))
+
+
+def ring_split(values, at):
+    rows = values.shape[0] // 4
+    return [lax.dynamic_slice_in_dim(values, lax.rem(at + j, 4) * rows, rows, 0) for j in range(4)]
 
 
 def gather(block):
@@ -277,6 +336,14 @@
 def by_place(place, first, second, axis=0):
     return jnp.where(
         place == 0, jnp.concatenate([first, second], axis), jnp.concatenate([second, first], axis)
+    )
+
+
+def other_half(values, place):
+    rows = values.shape[0] // 2
+    return (
+        lax.dynamic_slice_in_dim(values, (1 - place) * rows, rows, 0),
+        lax.dynamic_slice_in_dim(values, place * rows, rows, 0),
     )
 
 
@@ -300,7 +367,9 @@
 ):
     core = lax.axis_index("c")
     side = lax.axis_index("yl")
-    core_arg = core.astype(jnp.int32).reshape(1)
+    x_at, z_at, pair_at = lax.axis_index("x"), lax.axis_index("z"), lax.axis_index("yh")
+    y_at = lax.axis_index(RING_Y)
+    place = jnp.stack([core, x_at, y_at]).astype(jnp.int32)
     present = jnp.arange(SLOTS) < segment_counts[0]
     present_rows = jnp.repeat(present, HALFSEG)[:, None]
     cot = jnp.where(present_rows, cotangent.reshape(OWN, WIDTH), 0).astype(BF16)
@@ -318,11 +387,16 @@
 
     first, second = half_of(0), half_of(1)
     rows = lax.all_to_all(jnp.stack([first, first, second, second]), ("c", "yl"), 0, 0, tiled=True)
-    rows = rows.reshape(24, QKV + SMALL + HALF + UP)
-    near = halves_out(w_down)
-    down_rows = by_place(side, near, between_chips(near))
-
-    attn = gather(rows[:, : QKV + SMALL + HALF])
+    rows = rows.reshape(24, ATTN + UP)
+
+    attn = gather(rows[:, :ATTN])
+    ups = ring_order(ring_gather(rows[:, ATTN:], "z"), z_at)
+    ups = by_place(pair_at, ups, lax.ppermute(ups, "yh", [(0, 1), (1, 0)]))
+    ups = ring_gather(ups, "x")
+    downs = ring_order(ring_gather(halves_out(w_down), "x"), x_at)
+    downs = ring_order(ring_gather(downs, "z"), z_at)
+    downs = ring_gather(downs, RING_Y)
+
     w_in = attn[:, :QKV]
     small_all = attn[:, QKV : QKV + SMALL]
     own_out = attn[:, QKV + SMALL :]
@@ -337,89 +411,82 @@
 
     a1, qkv, own_o, lse = call(
         attend_kernel,
-        core_arg,
+        place,
         (x, vectors[0:1], vectors[1:2], w_in, qkv_b),
         (((ROWS, WIDTH), BF16), ((ROWS, QKV), BF16), ((ROWS, HALF), BF16), ((ROWS, 128), F32)),
     )
     far_o = between_cores(own_o)
-    w_up_all = gather(rows[:, QKV + SMALL + HALF :])
-    w_down_all = gather(down_rows)
-    hidden, m_own, m_far, grad_a_own, grad_up, grad_down, grad_up_b, grad_down_b = call(
+    hidden, m_own, m_far, grad_a_own, grad_up_b, grad_down_b, *grads = call(
         mlp_kernel,
-        core_arg,
-        (x, own_o, far_o, own_out, far_out, mid_vec, w_up_all, up_b, w_down_all, g),
+        place,
+        (x, own_o, far_o, own_out, far_out, mid_vec, up_b, g, *ups, *downs),
         (
             ((ROWS, WIDTH), F32),
             ((OWN, WIDTH), F32),
             ((OWN, WIDTH), F32),
             ((ROWS, WIDTH), F32),
-            ((WIDTH, UP), BF16),
-            ((UP, WIDTH), BF16),
             ((1, UP), F32),
             ((1, WIDTH), F32),
-        ),
+        )
+        + (((UP_ROWS, UP), BF16),) * 4
+        + (((DOWN_ROWS, WIDTH), BF16),) * 4,
+        (((WIDTH, UP), BF16), ((UP, WIDTH), BF16), ((WIDTH, UP), BF16), ((UP, WIDTH), BF16)),
     )
     grad_a_far = between_cores(grad_a_own)
     block = swap_items((m_own + between_cores(m_far)).astype(BF16))
     block_out = jnp.where(present_rows, block, 0).reshape(tokens.shape)
-
-    grad_w, grad_out, own_x, far_x, gh, vec_mid, grad_b = call(
+    up_cols = lax.dynamic_update_slice(jnp.zeros((WIDTH, 4), F32), grad_up_b.reshape(HALF, 4), (at, 0))
+    up_high = up_cols.astype(BF16).astype(F32)
+    up_cols = jnp.pad(up_high, ((0, 0), (8, SMALL - 12))) + jnp.pad(up_cols - up_high, ((0, 0), (24, SMALL - 28)))
+
+    gqkv, gh_low, own_x, far_x, gh, vec_mid = call(
         back_kernel,
-        core_arg,
-        (hidden, g, grad_a_own, grad_a_far, mid_vec, own_o, far_o, own_out, far_out, qkv, lse, a1, w_in),
+        place,
+        (hidden, g, grad_a_own, grad_a_far, mid_vec, own_out, far_out, qkv, lse, w_in),
         (
-            ((WIDTH, QKV), BF16),
-            ((WIDTH, HALF), BF16),
+            ((ROWS, QKV), BF16),
+            ((ROWS, WIDTH), BF16),
             ((OWN, WIDTH), F32),
             ((OWN, WIDTH), F32),
             ((OWN, WIDTH), F32),
             ((3, WIDTH), F32),
-            ((1, QKV), F32),
         ),
-        (((ROWS, WIDTH), BF16), ((ROWS, HALF), BF16), ((ROWS, QKV), BF16)),
-    )
-    grad_x, vec_first = call(
-        tokens_kernel,
-        None,
-        (x[:OWN], own_x, between_cores(far_x), gh, vectors[0:1]),
-        (((OWN, WIDTH), BF16), ((2, WIDTH), F32)),
+        (((ROWS, HALF), BF16),),
+    )
+    message, grad_x = call(
+        weights_kernel,
+        place,
+        (
+            x, a1, gqkv, own_o, far_o, gh_low, own_x, between_cores(far_x), gh, vectors[0:1], vec_mid, grad_down_b,
+            up_cols,
+        ),
+        (((WIDTH, ATTN), BF16), ((OWN, WIDTH), BF16)),
+        (((128, WIDTH), F32),),
     )
     grad_tokens = swap_items(grad_x).reshape(tokens.shape)
 
-    def placed(values, length):
-        return lax.dynamic_update_slice(jnp.zeros((1, length), F32), values, (0, core * values.shape[1]))
-
-    grad_vec = jnp.concatenate(
-        [
-            vec_first,
-            placed(grad_b[:, :HALF], WIDTH),
-            placed(grad_b[:, 2 * HALF :], WIDTH),
-            vec_mid,
-            grad_down_b,
-            placed(grad_up_b, FF).reshape(WIDTH, 4).T,
-        ],
-        axis=0,
-    ).T
-    high = grad_vec.astype(BF16)
-    low = (grad_vec - high.astype(F32)).astype(BF16)
-    grad_small = jnp.concatenate([high, low, jnp.zeros((WIDTH, SMALL - 24), BF16)], axis=1)
-
-    down_sum = reduce(grad_down)
-    down_near = jnp.where(side == 0, down_sum[:24], down_sum[24:])
-    down_other = jnp.where(side == 0, down_sum[24:], down_sum[:24])
-    out_down = halves_back(down_near + between_chips(down_other))
-    row_sum = jnp.concatenate(
-        [reduce(jnp.concatenate([grad_w, grad_small, grad_out], axis=1)), reduce(grad_up)], axis=1
-    )
-    got = lax.all_to_all(row_sum.reshape(4, 6, row_sum.shape[1]), ("c", "yl"), 0, 0, tiled=True)
+    up_sum = ring_reduce(grads[:4], "x").astype(BF16)
+    far_up, near_up = other_half(up_sum, pair_at)
+    up_sum = near_up.astype(F32) + lax.ppermute(far_up, "yh", [(0, 1), (1, 0)]).astype(F32)
+    up_sum = ring_reduce(ring_split(up_sum.astype(BF16), z_at), "z")
+    up_sum = jnp.swapaxes(up_sum.reshape(2, 2, 6, UP), 0, 1)
+    far_up, near_up = other_half(up_sum, side)
+    far_up, near_up = other_half(near_up[0] + between_chips(far_up)[0], core)
+    out_up = by_place(core, near_up[0], between_cores(far_up)[0], axis=1)
+
+    down_sum = ring_reduce(grads[4:], RING_Y).astype(BF16)
+    down_sum = ring_reduce(ring_split(down_sum, z_at), "z").astype(BF16)
+    down_sum = ring_reduce(ring_split(down_sum, x_at), "x")
+    out_down = halves_back(down_sum)
+
+    got = lax.all_to_all(reduce(message).reshape(4, 6, ATTN), ("c", "yl"), 0, 0, tiled=True)
     both = got[0::2] + got[1::2]
     out_qkv = jnp.concatenate(
         [both[t, :, j * HALF : (j + 1) * HALF] for j in range(3) for t in range(2)], axis=1
     )
     vec = both[0, :, QKV : QKV + SMALL] + both[1, :, QKV : QKV + SMALL]
-    vec = vec[:, :12] + vec[:, 12:24]
-    out_out = jnp.concatenate([both[t, :, QKV + SMALL : QKV + SMALL + HALF] for t in range(2)], axis=1)
-    out_up = jnp.concatenate([both[t, :, QKV + SMALL + HALF :] for t in range(2)], axis=1)
+    vec = vec[:, :12] + vec[:, 16:28]
+    out_out = jnp.concatenate([both[t, :, QKV + SMALL :] for t in range(2)], axis=1)
     return (
         block_out,
         grad_tokens,

time: 308 us -> 265 us (0.86)
  starting transfers between devices: 67.9 us -> 124 us
  waiting for transfers between devices: 112 us -> 71.2 us
  blocking collectives: 39.7 us -> 0 us
  local copies, waits for them, and re-layouts: 46.9 us -> 23.7 us
  other arithmetic: 8.96 us -> 13.8 us
    all_to_all x3 -> x1, waiting for transfers between devices: 74.4 us -> 0.01 us  [gather(): got = lax.all_to_all(spread, QUAD_AXES, 0, 0, tiled=True)]
    ppermute x0 -> x32, waiting for transfers between devices: none -> 67.2 us  [the longest x30 67.2 us: ring(): return lax.ppermute(values, axis, [(i, (i + by) % 4) for i in range(4)])]
    ppermute x0 -> x32, starting transfers between devices: none -> 67.2 us  [the longest x30 63 us: ring(): return lax.ppermute(values, axis, [(i, (i + by) % 4) for i in range(4)])]
    all_to_all x1 -> x0, blocking collectives: 39.7 us -> none  [reduce(): lax.all_to_all(grads.reshape(QUADS, rows, grads.shape[1]), QUAD_AXES, 0,...]
    ppermute x2 -> x1, waiting for transfers between devices: 25.1 us -> 1.23 us  [between_chips(): return lax.ppermute(values, 'yl', [(0, 1), (1, 0)])]
    all_to_all x3 -> x1, starting transfers between devices: 25.1 us -> 5 us  [gather(): got = lax.all_to_all(spread, QUAD_AXES, 0, 0, tiled=True)]
    ppermute x6 -> x7, starting transfers between devices: 5.24 us -> 17 us  [between_cores(): return lax.ppermute(values, 'c', [(0, 1), (1, 0)])]
    all_to_all x2 -> x1, starting transfers between devices: 13.9 us -> 5.63 us  [reduce(): lax.all_to_all(grads.reshape(QUADS, rows, grads.shape[1]), QUAD_AXES, 0,...]
  transfers between devices with their start and end apart: 20 -> 49, of which waited for: 8 -> 14; matrix products, arithmetic and copies ran while one was open for 15% -> 12% of each run, Pallas kernels for 5% -> 6%
where the time goes in v2:
time: 265 us; the launch traced here: 263 us
  starting transfers between devices  124 us (47%)
  waiting for transfers between devices  71.2 us (27%)
  Pallas kernels  28.2 us (11%)
  local copies, waits for them, and re-layouts  23.7 us (9%)
  other arithmetic  13.8 us (5%)
    ppermute x30, waiting for transfers between devices, ring(): return lax.ppermute(values, axis, [(i, (i + by) % 4) for i in range(4)])  67.2 us
    ppermute x30, starting transfers between devices, ring(): return lax.ppermute(values, axis, [(i, (i + by) % 4) for i in range(4)])  63 us
    pallas_call x4, Pallas kernels, call(): pl.pallas_call(kernel, out_shape=tuple((jax.ShapeDtypeStruct(s, d) for s,...  28.2 us
    ppermute x7, starting transfers between devices, between_cores(): return lax.ppermute(values, 'c', [(0, 1), (1, 0)])  17 us
    ppermute x3, starting transfers between devices, swap_items(): return lax.ppermute(values, ('c', 'yl'), [(0, 0), (1, 2), (2, 1), (3, 3)])  8.2 us
    ppermute x1, starting transfers between devices, halves_back(): return lax.ppermute(values, AXES, [(b, a) for a, b in HALVES])  6.75 us
    ppermute x1, starting transfers between devices, halves_out(): return lax.ppermute(values, AXES, HALVES)  6.17 us
    another operation x8, local copies, waits for them, and re-layouts, shards(): jnp.stack([ln1_gain, ln1_bias, q_bias, v_bias, out_bias, ln2_gain, ln2_bi...  6.03 us
  transfers between devices with their start and end apart: 49, of which 14 were waited for; matrix products, arithmetic and copies ran while one was open for 12% of the time, Pallas kernels for 6%

profile of v2, /device:TPU:1, one launch (start us, length us, event | category | flops | bytes accessed | tf_op | source)
XLA Modules:
  0.0 263.1 jit_solution(3659551183181511970)
XLA Ops:
  0.7 6.2 %collective-permute-start.11 = (bf16[24,768]{1,0:T(8,128)(2,1)}, bf16[24,768]{1,0:T(8,128)(2,1)S(1)}, u32[]{:S(2)}, u32[]{:S(2)}) collective-permute-start(bf16[24,768]{1,0:T(8,128)(2,1)} %param.29), channel_id=1, source_target_pairs={{0,0},{16,1},{64,2},{80,3},{4,4},{20,5},{68,6},{84,7},{8,8},{24,9}... | collective-permute-start | bytes 110600 | tf_op jit(solution)/shard_map/ppermute | solution.py:295
  16.1 3.4 %all-to-all-start = ((bf16[4,6,3200]{2,1,0:T(8,128)(2,1)}), bf16[4,6,3200]{2,1,0:T(8,128)(2,1)S(1)}, u32[]{:S(2)}, u32[]{:S(2)}) async-start(bf16[4,6,3200]{2,1,0:T(8,128)(2,1)} %pad_maximum_fusion.3), calls=%async_computation | async-start | bytes 409600 | tf_op jit(solution)/shard_map/all_to_all | solution.py:389
  21.2 2.7 %collective-permute-start = (bf16[128,1536]{1,0:T(8,128)(2,1)}, bf16[128,1536]{1,0:T(8,128)(2,1)}, u32[]{:S(2)}, u32[]{:S(2)}) collective-permute-start(bf16[128,1536]{1,0:T(8,128)(2,1)} %pad_maximum_fusion.1), channel_id=1, source_target_pairs={{0,0},{1,2},{2,1},{3,3},{4,4},{5,6},{6,5},{7,7},{8,8},{9,10},{10,9... | collective-permute-start | bytes 1179656 | tf_op jit(solution)/shard_map/ppermute | solution.py:281
  24.0 3.2 %collective-permute-start.12 = (bf16[24,768]{1,0:T(8,128)(2,1)S(1)}, bf16[24,768]{1,0:T(8,128)(2,1)S(1)}, u32[]{:S(2)}, u32[]{:S(2)}) collective-permute-start(bf16[24,768]{1,0:T(8,128)(2,1)S(1)} %collective-permute-done.11), channel_id=1, source_target_pairs={{0,96},{32,0},{64,32},{96,64},{1,97},{33,1},{65,33},{97,65},{2,98}... | collective-permute-start | bytes 110600 | tf_op jit(solution)/shard_map/ppermute | solution.py:303
  29.0 2.6 collective-permute-done.13
  32.5 3.8 %collective-permute-start.4 = (bf16[24,1536]{1,0:T(8,128)(2,1)S(1)}, bf16[24,1536]{1,0:T(8,128)(2,1)S(1)}, u32[]{:S(2)}, u32[]{:S(2)}) collective-permute-start(bf16[24,1536]{1,0:T(8,128)(2,1)S(1)} %slice.198), channel_id=1, source_target_pairs={{0,12},{4,0},{8,4},{12,8},{1,13},{5,1},{9,5},{13,9},{2,14},{6,2},{... | collective-permute-start | bytes 221192 | tf_op jit(solution)/shard_map/ppermute | solution.py:303
  37.1 2.0 collective-permute-start.15
  39.1 1.6 broadcast_in_dim.42
  40.7 5.0 %all-to-all-start.1 = ((bf16[32,24,1664]{2,1,0:T(8,128)(2,1)}), bf16[32,24,1664]{2,1,0:T(8,128)(2,1)S(1)}, u32[]{:S(2)}, u32[]{:S(2)}) async-start(bf16[32,24,1664]{2,1,0:T(8,128)(2,1)} %broadcast_in_dim.42), calls=%async_computation.1 | async-start | bytes 5111808 | tf_op jit(solution)/shard_map/all_to_all | solution.py:326
  45.8 2.8 %collective-permute-start.16 = (bf16[96,768]{1,0:T(8,128)(2,1)S(1)}, bf16[96,768]{1,0:T(8,128)(2,1)S(1)}, u32[]{:S(2)}, u32[]{:S(2)}) collective-permute-start(bf16[96,768]{1,0:T(8,128)(2,1)S(1)} %pad_maximum_fusion.4), channel_id=1, source_target_pairs={{0,8},{4,12},{8,0},{12,4},{1,9},{5,13},{9,1},{13,5},{2,10},{6,14},... | collective-permute-start | bytes 442376 | tf_op jit(solution)/shard_map/ppermute | solution.py:303
  49.1 2.8 %collective-permute-start.7 = (bf16[96,1536]{1,0:T(8,128)(2,1)S(1)}, bf16[96,1536]{1,0:T(8,128)(2,1)S(1)}, u32[]{:S(2)}, u32[]{:S(2)}) collective-permute-start(bf16[96,1536]{1,0:T(8,128)(2,1)S(1)} %pad_maximum_fusion.2), channel_id=1, source_target_pairs={{0,16},{16,0},{1,17},{17,1},{2,18},{18,2},{3,19},{19,3},{4,20},{20... | collective-permute-start | bytes 884744 | tf_op jit(solution)/shard_map/ppermute | solution.py:394
  51.9 23.4 %collective-permute-done.16 = bf16[96,768]{1,0:T(8,128)(2,1)S(1)} collective-permute-done((bf16[96,768]{1,0:T(8,128)(2,1)S(1)}, bf16[96,768]{1,0:T(8,128)(2,1)S(1)}, u32[]{:S(2)}, u32[]{:S(2)}) %collective-permute-start.16) | collective-permute-done | bytes 147488 | tf_op jit(solution)/shard_map/ppermute | solution.py:303
  75.2 5.8 %collective-permute-done.17 = bf16[96,768]{1,0:T(8,128)(2,1)S(1)} collective-permute-done((bf16[96,768]{1,0:T(8,128)(2,1)S(1)}, bf16[96,768]{1,0:T(8,128)(2,1)S(1)}, u32[]{:S(2)}, u32[]{:S(2)}) %collective-permute-start.17) | collective-permute-done | bytes 147488 | tf_op jit(solution)/shard_map/ppermute | solution.py:303
  82.2 5.1 %collective-permute-start.18 = (bf16[384,768]{1,0:T(8,128)(2,1)}, bf16[384,768]{1,0:T(8,128)(2,1)}, u32[]{:S(2)}, u32[]{:S(2)}) collective-permute-start(bf16[384,768]{1,0:T(8,128)(2,1)} %pad_maximum_fusion.down_0), channel_id=1, source_target_pairs={{0,17},{1,0},{16,1},{17,16},{2,19},{3,2},{18,3},{19,18},{4,21},{5,... | collective-permute-start | bytes 1769480 | tf_op jit(solution)/shard_map/ppermute | solution.py:303
  87.8 1.7 collective-permute-start.1
  91.6 1.5 collective-permute-start.10
  93.1 2.2 collective-permute-start.8
  99.5 14.6 %collective-permute-start.9 = (bf16[192,1536]{1,0:T(8,128)(2,1)}, bf16[192,1536]{1,0:T(8,128)(2,1)}, u32[]{:S(2)}, u32[]{:S(2)}) collective-permute-start(bf16[192,1536]{1,0:T(8,128)(2,1)} %broadcast_select_fusion.up_0), channel_id=1, source_target_pairs={{0,64},{32,96},{64,0},{96,32},{1,65},{33,97},{65,1},{97,33},{2,66}... | collective-permute-start | bytes 1769480 | tf_op jit(solution)/shard_map/ppermute | solution.py:303
  114.1 2.6 collective-permute-start.3
  117.3 4.3 %shard_map.271 = (bf16[256,768]{1,0:T(8,128)(2,1)}, bf16[256,1152]{1,0:T(8,128)(2,1)}, bf16[256,384]{1,0:T(8,128)(2,1)}, f32[256,128]{1,0:T(8,128)}) custom-call(s32[3]{0:T(128)} %pad_add_fusion.1.place_ref, bf16[256,768]{1,0:T(8,128)(2,1)} %get-tuple-element.84.x_ref, f32[1,768]{1,0:T(1,128)} %get-tuple-element.113.gain_ref, ...), custom_call_target="tpu_custom_call" | custom-call | tf_op jit(solution)/shard_map/pallas_call | solution.py:262
  123.4 1.7 collective-permute-done.9.up_2
  125.8 11.8 %shard_map.272 = (f32[256,768]{1,0:T(8,128)}, f32[128,768]{1,0:T(8,128)}, f32[128,768]{1,0:T(8,128)}, f32[256,768]{1,0:T(8,128)}, f32[1,1536]{1,0:T(1,128)}, /*i...) custom-call(s32[3]{0:T(128)} %pad_add_fusion.1.place_ref, ...), custom_call_target="tpu_custom_call" | custom-call | tf_op jit(solution)/shard_map/pallas_call | solution.py:262
  137.8 4.8 %collective-permute-start.36 = (bf16[384,768]{1,0:T(8,128)(2,1)}, bf16[384,768]{1,0:T(8,128)(2,1)S(1)}, u32[]{:S(2)}, u32[]{:S(2)}) collective-permute-start(bf16[384,768]{1,0:T(8,128)(2,1)} %get-tuple-element.65), channel_id=1, source_target_pairs={{0,16},{1,17},{16,0},{17,1},{2,18},{3,19},{18,2},{19,3},{4,20},{5,... | collective-permute-start | bytes 1769480 | tf_op jit(solution)/shard_map/ppermute | solution.py:303
  144.5 4.3 %collective-permute-start.21 = (f32[128,768]{1,0:T(8,128)}, f32[128,768]{1,0:T(8,128)S(1)}, u32[]{:S(2)}, u32[]{:S(2)}) collective-permute-start(f32[128,768]{1,0:T(8,128)} %get-tuple-element.43), channel_id=1, source_target_pairs={{0,2},{2,0},{1,3},{3,1},{4,6},{6,4},{5,7},{7,5},{8,10},{10,8},{9,1... | collective-permute-start | bytes 1179656 | tf_op jit(solution)/shard_map/ppermute | solution.py:273
  150.3 3.5 %collective-permute-start.27 = (bf16[192,1536]{1,0:T(8,128)(2,1)S(1)}, bf16[192,1536]{1,0:T(8,128)(2,1)S(1)}, u32[]{:S(2)}, u32[]{:S(2)}) collective-permute-start(bf16[192,1536]{1,0:T(8,128)(2,1)S(1)} %copy-done.12), channel_id=1, source_target_pairs={{0,64},{32,96},{64,0},{96,32},{1,65},{33,97},{65,1},{97,33},{2,66}... | collective-permute-start | bytes 1769480 | tf_op jit(solution)/shard_map/ppermute | solution.py:303
  153.9 2.2 collective-permute-start.28
  156.8 8.5 %collective-permute-done.36 = bf16[384,768]{1,0:T(8,128)(2,1)S(1)} collective-permute-done((bf16[384,768]{1,0:T(8,128)(2,1)}, bf16[384,768]{1,0:T(8,128)(2,1)S(1)}, u32[]{:S(2)}, u32[]{:S(2)}) %collective-permute-start.36) | collective-permute-done | bytes 589856 | tf_op jit(solution)/shard_map/ppermute | solution.py:303
  165.3 4.4 %collective-permute-start.23 = (f32[256,768]{1,0:T(8,128)S(1)}, f32[256,768]{1,0:T(8,128)S(1)}, u32[]{:S(2)}, u32[]{:S(2)}) collective-permute-start(f32[256,768]{1,0:T(8,128)S(1)} %copy-done.2), channel_id=1, source_target_pairs={{0,2},{2,0},{1,3},{3,1},{4,6},{6,4},{5,7},{7,5},{8,10},{10,8},{9,1... | collective-permute-start | bytes 2359304 | tf_op jit(solution)/shard_map/ppermute | solution.py:273
  169.7 1.9 collective-permute-start.22
  171.6 1.4 add_convert_fusion
  173.1 2.7 %collective-permute-start.38 = (bf16[96,768]{1,0:T(8,128)(2,1)S(1)}, bf16[96,768]{1,0:T(8,128)(2,1)S(1)}, u32[]{:S(2)}, u32[]{:S(2)}) collective-permute-start(bf16[96,768]{1,0:T(8,128)(2,1)S(1)} %get-tuple-element.85), channel_id=1, source_target_pairs={{0,4},{4,8},{8,12},{12,0},{1,5},{5,9},{9,13},{13,1},{2,6},{6,10},{... | collective-permute-start | bytes 442376 | tf_op jit(solution)/shard_map/ppermute | solution.py:303
  176.5 2.2 collective-permute-done.28
  178.8 1.7 collective-permute-start.40
  181.7 7.5 %shard_map.273 = (bf16[256,1152]{1,0:T(8,128)(2,1)}, bf16[256,768]{1,0:T(8,128)(2,1)}, f32[128,768]{1,0:T(8,128)}, f32[128,768]{1,0:T(8,128)}, f32[128,768]{1,0:T(8,128)}, /*index=5*/f32[3,768]{1,0:T(4,128)}) custom-call(s32[3]{0:T(128)} %pad_add_fusion.1.place_ref, f32[256,768]{1,0:T(8,128)} %get-tuple-element.45.h_ref, ...), custom_call_target="tpu_custom_call" | custom-call | tf_op jit(solution)/shard_map/pallas_call | solution.py:262
  189.2 1.5 collective-permute-start.24
  193.5 3.3 %collective-permute-start.42 = (bf16[24,768]{1,0:T(8,128)(2,1)}, bf16[24,768]{1,0:T(8,128)(2,1)}, u32[]{:S(2)}, u32[]{:S(2)}) collective-permute-start(bf16[24,768]{1,0:T(8,128)(2,1)} %get-tuple-element.101), channel_id=1, source_target_pairs={{0,64},{32,96},{64,0},{96,32},{1,65},{33,97},{65,1},{97,33},{2,66}... | collective-permute-start | bytes 110600 | tf_op jit(solution)/shard_map/ppermute | solution.py:303
  197.6 4.6 %shard_map.274 = (bf16[768,1664]{1,0:T(8,128)(2,1)}, bf16[128,768]{1,0:T(8,128)(2,1)}) custom-call(s32[3]{0:T(128)} %pad_add_fusion.1.place_ref, bf16[256,768]{1,0:T(8,128)(2,1)} %get-tuple-element.84.x_ref, bf16[256,768]{1,0:T(8,128)(2,1)} %get-tuple-element.44.a_ref, bf16[256,1152]{1,0:T(8,128)(2,1)} %get-tuple-element.49.gqkv_ref, ...), custom_call_target="tpu_custom_call" | custom-call | tf_op jit(solution)/shard_map/pallas_call | solution.py:262
  202.2 5.6 %all-to-all-start.2 = ((bf16[32,24,1664]{2,1,0:T(8,128)(2,1)}), bf16[32,24,1664]{2,1,0:T(8,128)(2,1)S(1)}, u32[]{:S(2)}, u32[]{:S(2)}) async-start(bf16[32,24,1664]{2,1,0:T(8,128)(2,1)} %bitcast.67), calls=%async_computation.2 | async-start | bytes 5111808 | tf_op jit(solution)/shard_map/all_to_all | solution.py:332
  210.2 2.4 collective-permute-start.31
  214.6 6.7 %collective-permute-start.44 = (f32[24,768]{1,0:T(8,128)S(1)}, f32[24,768]{1,0:T(8,128)S(1)}, u32[]{:S(2)}, u32[]{:S(2)}) collective-permute-start(f32[24,768]{1,0:T(8,128)S(1)} %convert_add_fusion.1), channel_id=1, source_target_pairs={{0,0},{1,16},{2,64},{3,80},{4,4},{5,20},{6,68},{7,84},{8,8},{9,24}... | collective-permute-start | bytes 221192 | tf_op jit(solution)/shard_map/ppermute | solution.py:299
  221.4 5.3 %collective-permute-done.30 = bf16[24,1536]{1,0:T(8,128)(2,1)S(1)} collective-permute-done((bf16[24,1536]{1,0:T(8,128)(2,1)S(1)}, bf16[24,1536]{1,0:T(8,128)(2,1)S(1)}, u32[]{:S(2)}, u32[]{:S(2)}) %collective-permute-start.30) | collective-permute-done | bytes 73760 | tf_op jit(solution)/shard_map/ppermute | solution.py:303
  226.7 5.4 %collective-permute-done.31 = bf16[24,1536]{1,0:T(8,128)(2,1)S(1)} collective-permute-done((bf16[24,1536]{1,0:T(8,128)(2,1)S(1)}, bf16[24,1536]{1,0:T(8,128)(2,1)S(1)}, u32[]{:S(2)}, u32[]{:S(2)}) %collective-permute-start.31) | collective-permute-done | bytes 73760 | tf_op jit(solution)/shard_map/ppermute | solution.py:303
  232.1 10.5 %collective-permute-done.32 = bf16[24,1536]{1,0:T(8,128)(2,1)S(1)} collective-permute-done((bf16[24,1536]{1,0:T(8,128)(2,1)S(1)}, bf16[24,1536]{1,0:T(8,128)(2,1)S(1)}, u32[]{:S(2)}, u32[]{:S(2)}) %collective-permute-start.32) | collective-permute-done | bytes 73760 | tf_op jit(solution)/shard_map/ppermute | solution.py:303
  242.6 1.6 collective-permute-start.33
  246.3 2.3 collective-permute-start.34
  248.5 3.5 %collective-permute-start.25 = (bf16[128,768]{1,0:T(8,128)(2,1)}, bf16[128,768]{1,0:T(8,128)(2,1)S(1)}, u32[]{:S(2)}, u32[]{:S(2)}) collective-permute-start(bf16[128,768]{1,0:T(8,128)(2,1)} %get-tuple-element.57), channel_id=1, source_target_pairs={{0,0},{1,2},{2,1},{3,3},{4,4},{5,6},{6,5},{7,7},{8,8},{9,10},{10,9... | collective-permute-start | bytes 589832 | tf_op jit(solution)/shard_map/ppermute | solution.py:281
  253.2 3.4 %all-to-all-start.3 = ((f32[4,6,1664]{2,1,0:T(8,128)}), f32[4,6,1664]{2,1,0:T(8,128)S(1)}, u32[]{:S(2)}, u32[]{:S(2)}) async-start(f32[4,6,1664]{2,1,0:T(8,128)} %reshape.96), calls=%async_computation.3 | async-start | bytes 425984 | tf_op jit(solution)/shard_map/all_to_all | solution.py:482
  257.2 2.3 all-to-all-done.3
  (181 shorter events, 46.7 us)
Async XLA Ops:
  0.7 23.3 %collective-permute-start.11 = (bf16[24,768]{1,0:T(8,128)(2,1)}, bf16[24,768]{1,0:T(8,128)(2,1)S(1)}, u32[]{:S(2)}, u32[]{:S(2)}) collective-permute-start(bf16[24,768]{1,0:T(8,128)(2,1)} %param.29), channel_id=1, source_target_pairs={{0,0},{16,1},{64,2},{80,3},{4,4},{20,5},{68,6},{84,7},{8,8},{24,9}... | collective-permute-start | bytes 110600 | tf_op jit(solution)/shard_map/ppermute | solution.py:295
  16.1 16.3 %all-to-all-start = ((bf16[4,6,3200]{2,1,0:T(8,128)(2,1)}), bf16[4,6,3200]{2,1,0:T(8,128)(2,1)S(1)}, u32[]{:S(2)}, u32[]{:S(2)}) async-start(bf16[4,6,3200]{2,1,0:T(8,128)(2,1)} %pad_maximum_fusion.3), calls=%async_computation | async-start | bytes 409600 | tf_op jit(solution)/shard_map/all_to_all | solution.py:389
  21.2 66.6 %collective-permute-start = (bf16[128,1536]{1,0:T(8,128)(2,1)}, bf16[128,1536]{1,0:T(8,128)(2,1)}, u32[]{:S(2)}, u32[]{:S(2)}) collective-permute-start(bf16[128,1536]{1,0:T(8,128)(2,1)} %pad_maximum_fusion.1), channel_id=1, source_target_pairs={{0,0},{1,2},{2,1},{3,3},{4,4},{5,6},{6,5},{7,7},{8,8},{9,10},{10,9... | collective-permute-start | bytes 1179656 | tf_op jit(solution)/shard_map/ppermute | solution.py:281
  24.0 5.0 %collective-permute-start.12 = (bf16[24,768]{1,0:T(8,128)(2,1)S(1)}, bf16[24,768]{1,0:T(8,128)(2,1)S(1)}, u32[]{:S(2)}, u32[]{:S(2)}) collective-permute-start(bf16[24,768]{1,0:T(8,128)(2,1)S(1)} %collective-permute-done.11), channel_id=1, source_target_pairs={{0,96},{32,0},{64,32},{96,64},{1,97},{33,1},{65,33},{97,65},{2,98}... | collective-permute-start | bytes 110600 | tf_op jit(solution)/shard_map/ppermute | solution.py:303
  27.2 4.3 %collective-permute-start.13 = (bf16[24,768]{1,0:T(8,128)(2,1)S(1)}, bf16[24,768]{1,0:T(8,128)(2,1)S(1)}, u32[]{:S(2)}, u32[]{:S(2)}) collective-permute-start(bf16[24,768]{1,0:T(8,128)(2,1)S(1)} %collective-permute-done.11), channel_id=1, source_target_pairs={{0,64},{32,96},{64,0},{96,32},{1,65},{33,97},{65,1},{97,33},{2,66}... | collective-permute-start | bytes 110600 | tf_op jit(solution)/shard_map/ppermute | solution.py:303
  28.4 4.0 %collective-permute-start.14 = (bf16[24,768]{1,0:T(8,128)(2,1)S(1)}, bf16[24,768]{1,0:T(8,128)(2,1)S(1)}, u32[]{:S(2)}, u32[]{:S(2)}) collective-permute-start(bf16[24,768]{1,0:T(8,128)(2,1)S(1)} %collective-permute-done.11), channel_id=1, source_target_pairs={{0,32},{32,64},{64,96},{96,0},{1,33},{33,65},{65,97},{97,1},{2,34}... | collective-permute-start | bytes 110600 | tf_op jit(solution)/shard_map/ppermute | solution.py:303
  32.5 13.2 %collective-permute-start.4 = (bf16[24,1536]{1,0:T(8,128)(2,1)S(1)}, bf16[24,1536]{1,0:T(8,128)(2,1)S(1)}, u32[]{:S(2)}, u32[]{:S(2)}) collective-permute-start(bf16[24,1536]{1,0:T(8,128)(2,1)S(1)} %slice.198), channel_id=1, source_target_pairs={{0,12},{4,0},{8,4},{12,8},{1,13},{5,1},{9,5},{13,9},{2,14},{6,2},{... | collective-permute-start | bytes 221192 | tf_op jit(solution)/shard_map/ppermute | solution.py:303
  36.3 12.2 %collective-permute-start.5 = (bf16[24,1536]{1,0:T(8,128)(2,1)S(1)}, bf16[24,1536]{1,0:T(8,128)(2,1)S(1)}, u32[]{:S(2)}, u32[]{:S(2)}) collective-permute-start(bf16[24,1536]{1,0:T(8,128)(2,1)S(1)} %slice.198), channel_id=1, source_target_pairs={{0,8},{4,12},{8,0},{12,4},{1,9},{5,13},{9,1},{13,5},{2,10},{6,14},... | collective-permute-start | bytes 221192 | tf_op jit(solution)/shard_map/ppermute | solution.py:303
  36.3 12.5 %collective-permute-start.6 = (bf16[24,1536]{1,0:T(8,128)(2,1)S(1)}, bf16[24,1536]{1,0:T(8,128)(2,1)S(1)}, u32[]{:S(2)}, u32[]{:S(2)}) collective-permute-start(bf16[24,1536]{1,0:T(8,128)(2,1)S(1)} %slice.198), channel_id=1, source_target_pairs={{0,4},{4,8},{8,12},{12,0},{1,5},{5,9},{9,13},{13,1},{2,6},{6,10},{... | collective-permute-start | bytes 221192 | tf_op jit(solution)/shard_map/ppermute | solution.py:303
  37.1 14.8 %collective-permute-start.15 = (bf16[96,768]{1,0:T(8,128)(2,1)S(1)}, bf16[96,768]{1,0:T(8,128)(2,1)S(1)}, u32[]{:S(2)}, u32[]{:S(2)}) collective-permute-start(bf16[96,768]{1,0:T(8,128)(2,1)S(1)} %pad_maximum_fusion.4), channel_id=1, source_target_pairs={{0,12},{4,0},{8,4},{12,8},{1,13},{5,1},{9,5},{13,9},{2,14},{6,2},{... | collective-permute-start | bytes 442376 | tf_op jit(solution)/shard_map/ppermute | solution.py:303
  40.7 55.5 %all-to-all-start.1 = ((bf16[32,24,1664]{2,1,0:T(8,128)(2,1)}), bf16[32,24,1664]{2,1,0:T(8,128)(2,1)S(1)}, u32[]{:S(2)}, u32[]{:S(2)}) async-start(bf16[32,24,1664]{2,1,0:T(8,128)(2,1)} %broadcast_in_dim.42), calls=%async_computation.1 | async-start | bytes 5111808 | tf_op jit(solution)/shard_map/all_to_all | solution.py:326
  45.8 29.5 %collective-permute-start.16 = (bf16[96,768]{1,0:T(8,128)(2,1)S(1)}, bf16[96,768]{1,0:T(8,128)(2,1)S(1)}, u32[]{:S(2)}, u32[]{:S(2)}) collective-permute-start(bf16[96,768]{1,0:T(8,128)(2,1)S(1)} %pad_maximum_fusion.4), channel_id=1, source_target_pairs={{0,8},{4,12},{8,0},{12,4},{1,9},{5,13},{9,1},{13,5},{2,10},{6,14},... | collective-permute-start | bytes 442376 | tf_op jit(solution)/shard_map/ppermute | solution.py:303
  48.6 32.5 %collective-permute-start.17 = (bf16[96,768]{1,0:T(8,128)(2,1)S(1)}, bf16[96,768]{1,0:T(8,128)(2,1)S(1)}, u32[]{:S(2)}, u32[]{:S(2)}) collective-permute-start(bf16[96,768]{1,0:T(8,128)(2,1)S(1)} %pad_maximum_fusion.4), channel_id=1, source_target_pairs={{0,4},{4,8},{8,12},{12,0},{1,5},{5,9},{9,13},{13,1},{2,6},{6,10},{... | collective-permute-start | bytes 442376 | tf_op jit(solution)/shard_map/ppermute | solution.py:303
  49.1 41.5 %collective-permute-start.7 = (bf16[96,1536]{1,0:T(8,128)(2,1)S(1)}, bf16[96,1536]{1,0:T(8,128)(2,1)S(1)}, u32[]{:S(2)}, u32[]{:S(2)}) collective-permute-start(bf16[96,1536]{1,0:T(8,128)(2,1)S(1)} %pad_maximum_fusion.2), channel_id=1, source_target_pairs={{0,16},{16,0},{1,17},{17,1},{2,18},{18,2},{3,19},{19,3},{4,20},{20... | collective-permute-start | bytes 884744 | tf_op jit(solution)/shard_map/ppermute | solution.py:394
  82.2 17.3 %collective-permute-start.18 = (bf16[384,768]{1,0:T(8,128)(2,1)}, bf16[384,768]{1,0:T(8,128)(2,1)}, u32[]{:S(2)}, u32[]{:S(2)}) collective-permute-start(bf16[384,768]{1,0:T(8,128)(2,1)} %pad_maximum_fusion.down_0), channel_id=1, source_target_pairs={{0,17},{1,0},{16,1},{17,16},{2,19},{3,2},{18,3},{19,18},{4,21},{5,... | collective-permute-start | bytes 1769480 | tf_op jit(solution)/shard_map/ppermute | solution.py:303
  87.2 26.8 %collective-permute-start.19 = (bf16[384,768]{1,0:T(8,128)(2,1)}, bf16[384,768]{1,0:T(8,128)(2,1)}, u32[]{:S(2)}, u32[]{:S(2)}) collective-permute-start(bf16[384,768]{1,0:T(8,128)(2,1)} %pad_maximum_fusion.down_0), channel_id=1, source_target_pairs={{0,16},{1,17},{16,0},{17,1},{2,18},{3,19},{18,2},{19,3},{4,20},{5,... | collective-permute-start | bytes 1769480 | tf_op jit(solution)/shard_map/ppermute | solution.py:303
  87.8 33.8 %collective-permute-start.20 = (bf16[384,768]{1,0:T(8,128)(2,1)}, bf16[384,768]{1,0:T(8,128)(2,1)}, u32[]{:S(2)}, u32[]{:S(2)}) collective-permute-start(bf16[384,768]{1,0:T(8,128)(2,1)} %pad_maximum_fusion.down_0), channel_id=1, source_target_pairs={{0,1},{1,16},{16,17},{17,0},{2,3},{3,18},{18,19},{19,2},{4,5},{5,2... | collective-permute-start | bytes 1769480 | tf_op jit(solution)/shard_map/ppermute | solution.py:303
  87.8 5.3 %collective-permute-start.1 = (bf16[128,1536]{1,0:T(8,128)(2,1)}, bf16[128,1536]{1,0:T(8,128)(2,1)S(1)}, u32[]{:S(2)}, u32[]{:S(2)}) collective-permute-start(bf16[128,1536]{1,0:T(8,128)(2,1)} %collective-permute-done), channel_id=1, source_target_pairs={{0,2},{2,0},{1,3},{3,1},{4,6},{6,4},{5,7},{7,5},{8,10},{10,8},{9,1... | collective-permute-start | bytes 1179656 | tf_op jit(solution)/shard_map/ppermute | solution.py:273
  91.6 31.8 %collective-permute-start.10 = (bf16[192,1536]{1,0:T(8,128)(2,1)}, bf16[192,1536]{1,0:T(8,128)(2,1)}, u32[]{:S(2)}, u32[]{:S(2)}) collective-permute-start(bf16[192,1536]{1,0:T(8,128)(2,1)} %broadcast_select_fusion.up_0), channel_id=1, source_target_pairs={{0,32},{32,64},{64,96},{96,0},{1,33},{33,65},{65,97},{97,1},{2,34}... | collective-permute-start | bytes 1769480 | tf_op jit(solution)/shard_map/ppermute | solution.py:303
  93.1 30.3 %collective-permute-start.8 = (bf16[192,1536]{1,0:T(8,128)(2,1)}, bf16[192,1536]{1,0:T(8,128)(2,1)}, u32[]{:S(2)}, u32[]{:S(2)}) collective-permute-start(bf16[192,1536]{1,0:T(8,128)(2,1)} %broadcast_select_fusion.up_0), channel_id=1, source_target_pairs={{0,96},{32,0},{64,32},{96,64},{1,97},{33,1},{65,33},{97,65},{2,98}... | collective-permute-start | bytes 1769480 | tf_op jit(solution)/shard_map/ppermute | solution.py:303
  99.5 25.6 %collective-permute-start.9 = (bf16[192,1536]{1,0:T(8,128)(2,1)}, bf16[192,1536]{1,0:T(8,128)(2,1)}, u32[]{:S(2)}, u32[]{:S(2)}) collective-permute-start(bf16[192,1536]{1,0:T(8,128)(2,1)} %broadcast_select_fusion.up_0), channel_id=1, source_target_pairs={{0,64},{32,96},{64,0},{96,32},{1,65},{33,97},{65,1},{97,33},{2,66}... | collective-permute-start | bytes 1769480 | tf_op jit(solution)/shard_map/ppermute | solution.py:303
  114.1 11.0 %collective-permute-start.3 = (bf16[768,384]{1,0:T(8,128)(2,1)S(1)}, bf16[768,384]{1,0:T(8,128)(2,1)}, u32[]{:S(2)}, u32[]{:S(2)}) collective-permute-start(bf16[768,384]{1,0:T(8,128)(2,1)S(1)} %slice.194.own_out_ref), channel_id=1, source_target_pairs={{0,2},{2,0},{1,3},{3,1},{4,6},{6,4},{5,7},{7,5},{8,10},{10,8},{9,1... | collective-permute-start | bytes 1769480 | tf_op jit(solution)/shard_map/ppermute | solution.py:273
  137.6 16.3 %collective-permute-start.35 = (bf16[384,768]{1,0:T(8,128)(2,1)}, bf16[384,768]{1,0:T(8,128)(2,1)S(1)}, u32[]{:S(2)}, u32[]{:S(2)}) collective-permute-start(bf16[384,768]{1,0:T(8,128)(2,1)} %get-tuple-element.64), channel_id=1, source_target_pairs={{0,1},{1,16},{16,17},{17,0},{2,3},{3,18},{18,19},{19,2},{4,5},{5,2... | collective-permute-start | bytes 1769480 | tf_op jit(solution)/shard_map/ppermute | solution.py:303
  137.8 27.6 %collective-permute-start.36 = (bf16[384,768]{1,0:T(8,128)(2,1)}, bf16[384,768]{1,0:T(8,128)(2,1)S(1)}, u32[]{:S(2)}, u32[]{:S(2)}) collective-permute-start(bf16[384,768]{1,0:T(8,128)(2,1)} %get-tuple-element.65), channel_id=1, source_target_pairs={{0,16},{1,17},{16,0},{17,1},{2,18},{3,19},{18,2},{19,3},{4,20},{5,... | collective-permute-start | bytes 1769480 | tf_op jit(solution)/shard_map/ppermute | solution.py:303
  142.6 27.1 %collective-permute-start.37 = (bf16[384,768]{1,0:T(8,128)(2,1)}, bf16[384,768]{1,0:T(8,128)(2,1)}, u32[]{:S(2)}, u32[]{:S(2)}) collective-permute-start(bf16[384,768]{1,0:T(8,128)(2,1)} %get-tuple-element.66), channel_id=1, source_target_pairs={{0,17},{1,0},{16,1},{17,16},{2,19},{3,2},{18,3},{19,18},{4,21},{5,... | collective-permute-start | bytes 1769480 | tf_op jit(solution)/shard_map/ppermute | solution.py:303
  142.6 30.5 %collective-permute-start.26 = (bf16[192,1536]{1,0:T(8,128)(2,1)}, bf16[192,1536]{1,0:T(8,128)(2,1)S(1)}, u32[]{:S(2)}, u32[]{:S(2)}) collective-permute-start(bf16[192,1536]{1,0:T(8,128)(2,1)} %get-tuple-element.60), channel_id=1, source_target_pairs={{0,32},{32,64},{64,96},{96,0},{1,33},{33,65},{65,97},{97,1},{2,34}... | collective-permute-start | bytes 1769480 | tf_op jit(solution)/shard_map/ppermute | solution.py:303
  144.5 5.8 %collective-permute-start.21 = (f32[128,768]{1,0:T(8,128)}, f32[128,768]{1,0:T(8,128)S(1)}, u32[]{:S(2)}, u32[]{:S(2)}) collective-permute-start(f32[128,768]{1,0:T(8,128)} %get-tuple-element.43), channel_id=1, source_target_pairs={{0,2},{2,0},{1,3},{3,1},{4,6},{6,4},{5,7},{7,5},{8,10},{10,8},{9,1... | collective-permute-start | bytes 1179656 | tf_op jit(solution)/shard_map/ppermute | solution.py:273
  150.3 25.4 %collective-permute-start.27 = (bf16[192,1536]{1,0:T(8,128)(2,1)S(1)}, bf16[192,1536]{1,0:T(8,128)(2,1)S(1)}, u32[]{:S(2)}, u32[]{:S(2)}) collective-permute-start(bf16[192,1536]{1,0:T(8,128)(2,1)S(1)} %copy-done.12), channel_id=1, source_target_pairs={{0,64},{32,96},{64,0},{96,32},{1,65},{33,97},{65,1},{97,33},{2,66}... | collective-permute-start | bytes 1769480 | tf_op jit(solution)/shard_map/ppermute | solution.py:303
  153.9 24.9 %collective-permute-start.28 = (bf16[192,1536]{1,0:T(8,128)(2,1)S(1)}, bf16[192,1536]{1,0:T(8,128)(2,1)S(1)}, u32[]{:S(2)}, u32[]{:S(2)}) collective-permute-start(bf16[192,1536]{1,0:T(8,128)(2,1)S(1)} %copy-done.11), channel_id=1, source_target_pairs={{0,96},{32,0},{64,32},{96,64},{1,97},{33,1},{65,33},{97,65},{2,98}... | collective-permute-start | bytes 1769480 | tf_op jit(solution)/shard_map/ppermute | solution.py:303
  165.3 15.4 %collective-permute-start.23 = (f32[256,768]{1,0:T(8,128)S(1)}, f32[256,768]{1,0:T(8,128)S(1)}, u32[]{:S(2)}, u32[]{:S(2)}) collective-permute-start(f32[256,768]{1,0:T(8,128)S(1)} %copy-done.2), channel_id=1, source_target_pairs={{0,2},{2,0},{1,3},{3,1},{4,6},{6,4},{5,7},{7,5},{8,10},{10,8},{9,1... | collective-permute-start | bytes 2359304 | tf_op jit(solution)/shard_map/ppermute | solution.py:273
  169.7 74.5 %collective-permute-start.22 = (bf16[128,768]{1,0:T(8,128)(2,1)}, bf16[128,768]{1,0:T(8,128)(2,1)S(1)}, u32[]{:S(2)}, u32[]{:S(2)}) collective-permute-start(bf16[128,768]{1,0:T(8,128)(2,1)} %add_convert_fusion.3), channel_id=1, source_target_pairs={{0,0},{1,2},{2,1},{3,3},{4,4},{5,6},{6,5},{7,7},{8,8},{9,10},{10,9... | collective-permute-start | bytes 589832 | tf_op jit(solution)/shard_map/ppermute | solution.py:281
  173.1 18.3 %collective-permute-start.38 = (bf16[96,768]{1,0:T(8,128)(2,1)S(1)}, bf16[96,768]{1,0:T(8,128)(2,1)S(1)}, u32[]{:S(2)}, u32[]{:S(2)}) collective-permute-start(bf16[96,768]{1,0:T(8,128)(2,1)S(1)} %get-tuple-element.85), channel_id=1, source_target_pairs={{0,4},{4,8},{8,12},{12,0},{1,5},{5,9},{9,13},{13,1},{2,6},{6,10},{... | collective-permute-start | bytes 442376 | tf_op jit(solution)/shard_map/ppermute | solution.py:303
  175.7 17.0 %collective-permute-start.39 = (bf16[96,768]{1,0:T(8,128)(2,1)S(1)}, bf16[96,768]{1,0:T(8,128)(2,1)S(1)}, u32[]{:S(2)}, u32[]{:S(2)}) collective-permute-start(bf16[96,768]{1,0:T(8,128)(2,1)S(1)} %get-tuple-element.87), channel_id=1, source_target_pairs={{0,8},{4,12},{8,0},{12,4},{1,9},{5,13},{9,1},{13,5},{2,10},{6,14},... | collective-permute-start | bytes 442376 | tf_op jit(solution)/shard_map/ppermute | solution.py:303
  178.8 14.0 %collective-permute-start.40 = (bf16[96,768]{1,0:T(8,128)(2,1)S(1)}, bf16[96,768]{1,0:T(8,128)(2,1)S(1)}, u32[]{:S(2)}, u32[]{:S(2)}) collective-permute-start(bf16[96,768]{1,0:T(8,128)(2,1)S(1)} %get-tuple-element.86), channel_id=1, source_target_pairs={{0,12},{4,0},{8,4},{12,8},{1,13},{5,1},{9,5},{13,9},{2,14},{6,2},{... | collective-permute-start | bytes 442376 | tf_op jit(solution)/shard_map/ppermute | solution.py:303
  189.2 7.7 %collective-permute-start.24 = (f32[128,768]{1,0:T(8,128)}, f32[128,768]{1,0:T(8,128)S(1)}, u32[]{:S(2)}, u32[]{:S(2)}) collective-permute-start(f32[128,768]{1,0:T(8,128)} %get-tuple-element.52), channel_id=1, source_target_pairs={{0,2},{2,0},{1,3},{3,1},{4,6},{6,4},{5,7},{7,5},{8,10},{10,8},{9,1... | collective-permute-start | bytes 1179656 | tf_op jit(solution)/shard_map/ppermute | solution.py:273
  191.4 16.4 %collective-permute-start.29 = (bf16[96,1536]{1,0:T(8,128)(2,1)}, bf16[96,1536]{1,0:T(8,128)(2,1)}, u32[]{:S(2)}, u32[]{:S(2)}) collective-permute-start(bf16[96,1536]{1,0:T(8,128)(2,1)} %constant_dynamic-slice_fusion.10), channel_id=1, source_target_pairs={{0,16},{16,0},{1,17},{17,1},{2,18},{18,2},{3,19},{19,3},{4,20},{20... | collective-permute-start | bytes 884744 | tf_op jit(solution)/shard_map/ppermute | solution.py:470
  193.5 16.7 %collective-permute-start.41 = (bf16[24,768]{1,0:T(8,128)(2,1)}, bf16[24,768]{1,0:T(8,128)(2,1)}, u32[]{:S(2)}, u32[]{:S(2)}) collective-permute-start(bf16[24,768]{1,0:T(8,128)(2,1)} %get-tuple-element.99), channel_id=1, source_target_pairs={{0,32},{32,64},{64,96},{96,0},{1,33},{33,65},{65,97},{97,1},{2,34}... | collective-permute-start | bytes 110600 | tf_op jit(solution)/shard_map/ppermute | solution.py:303
  193.5 19.1 %collective-permute-start.42 = (bf16[24,768]{1,0:T(8,128)(2,1)}, bf16[24,768]{1,0:T(8,128)(2,1)}, u32[]{:S(2)}, u32[]{:S(2)}) collective-permute-start(bf16[24,768]{1,0:T(8,128)(2,1)} %get-tuple-element.101), channel_id=1, source_target_pairs={{0,64},{32,96},{64,0},{96,32},{1,65},{33,97},{65,1},{97,33},{2,66}... | collective-permute-start | bytes 110600 | tf_op jit(solution)/shard_map/ppermute | solution.py:303
  196.8 17.0 %collective-permute-start.43 = (bf16[24,768]{1,0:T(8,128)(2,1)S(1)}, bf16[24,768]{1,0:T(8,128)(2,1)}, u32[]{:S(2)}, u32[]{:S(2)}) collective-permute-start(bf16[24,768]{1,0:T(8,128)(2,1)S(1)} %get-tuple-element.100), channel_id=1, source_target_pairs={{0,96},{32,0},{64,32},{96,64},{1,97},{33,1},{65,33},{97,65},{2,98}... | collective-permute-start | bytes 110600 | tf_op jit(solution)/shard_map/ppermute | solution.py:303
  202.2 49.9 %all-to-all-start.2 = ((bf16[32,24,1664]{2,1,0:T(8,128)(2,1)}), bf16[32,24,1664]{2,1,0:T(8,128)(2,1)S(1)}, u32[]{:S(2)}, u32[]{:S(2)}) async-start(bf16[32,24,1664]{2,1,0:T(8,128)(2,1)} %bitcast.67), calls=%async_computation.2 | async-start | bytes 5111808 | tf_op jit(solution)/shard_map/all_to_all | solution.py:332
  208.9 17.8 %collective-permute-start.30 = (bf16[24,1536]{1,0:T(8,128)(2,1)S(1)}, bf16[24,1536]{1,0:T(8,128)(2,1)S(1)}, u32[]{:S(2)}, u32[]{:S(2)}) collective-permute-start(bf16[24,1536]{1,0:T(8,128)(2,1)S(1)} %get-tuple-element.94), channel_id=1, source_target_pairs={{0,4},{4,8},{8,12},{12,0},{1,5},{5,9},{9,13},{13,1},{2,6},{6,10},{... | collective-permute-start | bytes 221192 | tf_op jit(solution)/shard_map/ppermute | solution.py:303
  210.2 21.9 %collective-permute-start.31 = (bf16[24,1536]{1,0:T(8,128)(2,1)S(1)}, bf16[24,1536]{1,0:T(8,128)(2,1)S(1)}, u32[]{:S(2)}, u32[]{:S(2)}) collective-permute-start(bf16[24,1536]{1,0:T(8,128)(2,1)S(1)} %get-tuple-element.96), channel_id=1, source_target_pairs={{0,8},{4,12},{8,0},{12,4},{1,9},{5,13},{9,1},{13,5},{2,10},{6,14},... | collective-permute-start | bytes 221192 | tf_op jit(solution)/shard_map/ppermute | solution.py:303
  212.6 29.9 %collective-permute-start.32 = (bf16[24,1536]{1,0:T(8,128)(2,1)S(1)}, bf16[24,1536]{1,0:T(8,128)(2,1)S(1)}, u32[]{:S(2)}, u32[]{:S(2)}) collective-permute-start(bf16[24,1536]{1,0:T(8,128)(2,1)S(1)} %get-tuple-element.95), channel_id=1, source_target_pairs={{0,12},{4,0},{8,4},{12,8},{1,13},{5,1},{9,5},{13,9},{2,14},{6,2},{... | collective-permute-start | bytes 221192 | tf_op jit(solution)/shard_map/ppermute | solution.py:303
  214.6 30.4 %collective-permute-start.44 = (f32[24,768]{1,0:T(8,128)S(1)}, f32[24,768]{1,0:T(8,128)S(1)}, u32[]{:S(2)}, u32[]{:S(2)}) collective-permute-start(f32[24,768]{1,0:T(8,128)S(1)} %convert_add_fusion.1), channel_id=1, source_target_pairs={{0,0},{1,16},{2,64},{3,80},{4,4},{5,20},{6,68},{7,84},{8,8},{9,24}... | collective-permute-start | bytes 221192 | tf_op jit(solution)/shard_map/ppermute | solution.py:299
  242.6 3.6 %collective-permute-start.33 = (f32[1,2,6,1536]{3,2,1,0:T(8,128)S(1)}, f32[1,2,6,1536]{3,2,1,0:T(8,128)S(1)}, u32[]{:S(2)}, u32[]{:S(2)}) collective-permute-start(f32[1,2,6,1536]{3,2,1,0:T(8,128)S(1)} %dynamic-slice_bitcast_fusion), channel_id=1, source_target_pairs={{0,1},{1,0},{2,3},{3,2},{4,5},{5,4},{6,7},{7,6},{8,9},{9,8},{10,11... | collective-permute-start | bytes 221192 | tf_op jit(solution)/shard_map/ppermute | solution.py:277
  246.3 10.3 %collective-permute-start.34 = (f32[1,6,1536]{2,1,0:T(8,128)S(1)}, f32[1,6,1536]{2,1,0:T(8,128)S(1)}, u32[]{:S(2)}, u32[]{:S(2)}) collective-permute-start(f32[1,6,1536]{2,1,0:T(8,128)S(1)} %get-tuple-element.109), channel_id=1, source_target_pairs={{0,2},{2,0},{1,3},{3,1},{4,6},{6,4},{5,7},{7,5},{8,10},{10,8},{9,1... | collective-permute-start | bytes 110600 | tf_op jit(solution)/shard_map/ppermute | solution.py:273
  248.5 8.7 %collective-permute-start.25 = (bf16[128,768]{1,0:T(8,128)(2,1)}, bf16[128,768]{1,0:T(8,128)(2,1)S(1)}, u32[]{:S(2)}, u32[]{:S(2)}) collective-permute-start(bf16[128,768]{1,0:T(8,128)(2,1)} %get-tuple-element.57), channel_id=1, source_target_pairs={{0,0},{1,2},{2,1},{3,3},{4,4},{5,6},{6,5},{7,7},{8,8},{9,10},{10,9... | collective-permute-start | bytes 589832 | tf_op jit(solution)/shard_map/ppermute | solution.py:281
  253.2 6.4 %all-to-all-start.3 = ((f32[4,6,1664]{2,1,0:T(8,128)}), f32[4,6,1664]{2,1,0:T(8,128)S(1)}, u32[]{:S(2)}, u32[]{:S(2)}) async-start(f32[4,6,1664]{2,1,0:T(8,128)} %reshape.96), calls=%async_computation.3 | async-start | bytes 425984 | tf_op jit(solution)/shard_map/all_to_all | solution.py:482
  (14 other events, 132.1 us)
